TPU v7x, 32 devices: a whole 2x2x4 slice. The times are simulated.
32 devices in a mesh: dp: 16 (over z, y, x), tensor: 2 (over core).
Axes of the slice: x: 2, y: 2, z: 4, core: 2. Of those that a mesh axis runs over, the one named last changes fastest.
Arguments:
- question_tokens: bfloat16 [32, 64, 768], P('dp'), may hold values from -6 to 6
- passage_tokens: bfloat16 [32, 256, 768], P('dp'), may hold values from -6 to 6
- question_cotangent: bfloat16 [32, 64, 768], P('dp'), may hold values from -6 to 6
- passage_cotangent: bfloat16 [32, 256, 768], P('dp'), may hold values from -6 to 6
- question_lengths: int32 [32], P('dp'), may hold values from 16 to 64, as said below
- passage_lengths: int32 [32], P('dp'), may hold values from 64 to 256, as said below
- dataset_ids: int32 [32], replicated, may hold values from 0 to 3
- positives: int32 [32], replicated, may hold values from 0 to 31, as said below
- attn_in: bfloat16 [2, 768, 3, 768], P(None, None, None, 'tensor'), may hold values from -0.21875 to 0.21875
- attn_in_bias: bfloat16 [2, 2, 768], P(None, None, 'tensor'), may hold values from -3 to 3
- attn_out: bfloat16 [2, 768, 768], P(None, 'tensor'), may hold values from -0.875 to 0.875
- ffn_in: bfloat16 [2, 768, 3072], P(None, None, 'tensor'), may hold values from -0.21875 to 0.21875
- ffn_in_bias: bfloat16 [2, 3072], P(None, 'tensor'), may hold values from -3 to 3
- ffn_out: bfloat16 [2, 3072, 768], P(None, 'tensor'), may hold values from -0.109375 to 0.109375
- out_biases: bfloat16 [2, 2, 768], replicated, may hold values from -2 to 2
- norm_gains: bfloat16 [2, 2, 768], replicated, may hold values from 0.25 to 1.75
- norm_shifts: bfloat16 [2, 2, 768], replicated, may hold values from -2 to 2
Outputs:
- question_out: bfloat16 [32, 64, 768], P('dp')
- passage_out: bfloat16 [32, 256, 768], P('dp')
- contrastive_loss: float32 [], replicated
- question_grad: bfloat16 [32, 64, 768], P('dp')
- passage_grad: bfloat16 [32, 256, 768], P('dp')
- grad_attn_in: float32 [2, 768, 3, 768], P(None, 'dp', None, 'tensor')
- grad_attn_in_bias: float32 [2, 2, 768], P(None, None, ('tensor', 'dp'))
- grad_attn_out: float32 [2, 768, 768], P(None, 'tensor', 'dp')
- grad_ffn_in: float32 [2, 768, 3072], P(None, 'dp', 'tensor')
- grad_ffn_in_bias: float32 [2, 3072], P(None, ('tensor', 'dp'))
- grad_ffn_out: float32 [2, 3072, 768], P(None, 'tensor', 'dp')
- grad_out_biases: float32 [2, 2, 768], P(None, None, 'dp')
- grad_norm_gains: float32 [2, 2, 768], P(None, None, 'dp')
- grad_norm_shifts: float32 [2, 2, 768], P(None, None, 'dp')
Inputs may be any that keep to these rules, and one draw needn't show every extreme that they name: `question_lengths`: some question has 64 real tokens and some has 16. `passage_lengths`: some passage has 256 real tokens and some has 64. `positives`: a permutation of the groups.
All inputs are finite; a program needn't handle non-finite values.
Results may differ from a plain program's by a relative error of at most 0.019.
Values may be sent and summed in bfloat16 or wider, within the bound.
A program may use at most 192 MiB of HBM per device.

v0:
```python
from functools import partial

import jax
import jax.numpy as jnp
from jax import lax
from jax.sharding import PartitionSpec as P

D = 768
HD = 64


EPSILON = 1e-06
NEGATIVE = -1e30
HIGHEST = lax.Precision.HIGHEST
score_gain = 3.0


def norm_forward(summed, scale_row, shift_row):
    row_mean = jnp.mean(summed, axis=-1, keepdims=True)
    centred = summed - row_mean
    inv_std = lax.rsqrt(jnp.mean(centred * centred, axis=-1, keepdims=True) + EPSILON)
    normed = centred * inv_std
    return (normed * scale_row + shift_row, normed, inv_std)


def norm_backward(incoming, normed, inv_std, scale_row):
    scaled = incoming * scale_row
    outgoing = inv_std * (
        scaled
        - jnp.mean(scaled, axis=-1, keepdims=True)
        - normed * jnp.mean(scaled * normed, axis=-1, keepdims=True)
    )
    return (outgoing, jnp.sum(incoming * normed, axis=(0, 1)), jnp.sum(incoming, axis=(0, 1)))


def key_visible(lengths, length):
    positions = jnp.arange(length, dtype=jnp.int32)
    return (positions[None, :] < lengths[:, None])[:, None, None, :]


def head_scores(queries, key_rows, visible):
    raw_scores = jnp.einsum(
        "bqhe,bkhe->bhqk", queries, key_rows, preferred_element_type=jnp.float32
    ) * HD ** (-0.5)
    return jnp.where(visible, raw_scores, NEGATIVE)


def split_heads(matrix):
    return matrix.reshape(matrix.shape[0], matrix.shape[1], matrix.shape[2] // HD, HD)


def join_heads(per_head):
    return per_head.reshape(
        per_head.shape[0], per_head.shape[1], per_head.shape[2] * per_head.shape[3]
    )


def encoder_forward(tokens, lengths, params):
    (
        attn_in,
        attn_in_bias,
        attn_out,
        ffn_in,
        ffn_in_bias,
        ffn_out,
        out_biases,
        norm_gains,
        norm_shifts,
    ) = params
    projected = jnp.einsum("bld,dce->blce", tokens, attn_in, preferred_element_type=jnp.float32)
    in_bias = attn_in_bias.astype(jnp.float32)
    queries = split_heads((projected[:, :, 0] + in_bias[0]).astype(jnp.bfloat16))
    key_rows = split_heads(projected[:, :, 1].astype(jnp.bfloat16))
    values = split_heads((projected[:, :, 2] + in_bias[1]).astype(jnp.bfloat16))
    visible = key_visible(lengths, tokens.shape[1])
    scores = head_scores(queries, key_rows, visible)
    row_top = jnp.max(scores, axis=-1, keepdims=True)
    log_total = row_top + jnp.log(jnp.sum(jnp.exp(scores - row_top), axis=-1, keepdims=True))
    attn_probs = jnp.exp(scores - log_total).astype(jnp.bfloat16)
    context = join_heads(
        jnp.einsum(
            "bhqk,bkhe->bqhe", attn_probs, values, preferred_element_type=jnp.float32
        ).astype(jnp.bfloat16)
    )
    attn_part = jnp.einsum("ble,ed->bld", context, attn_out, preferred_element_type=jnp.float32)
    attn_sum = lax.psum(attn_part.astype(jnp.bfloat16), "tensor").astype(jnp.float32)
    bias_rows = out_biases.astype(jnp.float32)
    gain_rows = norm_gains.astype(jnp.float32)
    shift_rows = norm_shifts.astype(jnp.float32)
    hidden_float, normed_first, inv_first = norm_forward(
        tokens.astype(jnp.float32) + attn_sum + bias_rows[0], gain_rows[0], shift_rows[0]
    )
    hidden = hidden_float.astype(jnp.bfloat16)
    up_pre = jnp.einsum(
        "bld,df->blf", hidden, ffn_in, preferred_element_type=jnp.float32
    ) + ffn_in_bias.astype(jnp.float32)
    activated = jax.nn.gelu(up_pre, approximate=False).astype(jnp.bfloat16)
    down_part = jnp.einsum("blf,fd->bld", activated, ffn_out, preferred_element_type=jnp.float32)
    down_sum = lax.psum(down_part.astype(jnp.bfloat16), "tensor").astype(jnp.float32)
    outputs, normed_second, inv_second = norm_forward(
        hidden.astype(jnp.float32) + down_sum + bias_rows[1], gain_rows[1], shift_rows[1]
    )
    saved = (
        tokens,
        queries,
        key_rows,
        values,
        log_total,
        context,
        normed_first,
        inv_first,
        hidden,
        up_pre,
        activated,
        normed_second,
        inv_second,
    )
    return (outputs, saved)


def encoder_backward(incoming, saved, lengths, params):
    (
        attn_in,
        attn_in_bias,
        attn_out,
        ffn_in,
        ffn_in_bias,
        ffn_out,
        out_biases,
        norm_gains,
        norm_shifts,
    ) = params
    (
        tokens,
        queries,
        key_rows,
        values,
        log_total,
        context,
        normed_first,
        inv_first,
        hidden,
        up_pre,
        activated,
        normed_second,
        inv_second,
    ) = saved
    groups_here, length, model_width = tokens.shape
    gain_rows = norm_gains.astype(jnp.float32)
    d_second, gain_second, shift_second = norm_backward(
        incoming, normed_second, inv_second, gain_rows[1]
    )
    d_down = d_second.astype(jnp.bfloat16)
    grad_ffn_out = jnp.einsum("blf,bld->fd", activated, d_down, preferred_element_type=jnp.float32)
    d_activated = jnp.einsum("bld,fd->blf", d_down, ffn_out, preferred_element_type=jnp.float32)
    gelu_pull = jax.vjp(partial(jax.nn.gelu, approximate=False), up_pre)[1]
    d_up = gelu_pull(d_activated)[0].astype(jnp.bfloat16)
    grad_ffn_in = jnp.einsum("bld,blf->df", hidden, d_up, preferred_element_type=jnp.float32)
    hidden_part = jnp.einsum("blf,df->bld", d_up, ffn_in, preferred_element_type=jnp.float32)
    d_hidden = d_second + lax.psum(hidden_part.astype(jnp.bfloat16), "tensor").astype(jnp.float32)
    d_first, gain_first, shift_first = norm_backward(
        d_hidden, normed_first, inv_first, gain_rows[0]
    )
    d_attn = d_first.astype(jnp.bfloat16)
    grad_attn_out = jnp.einsum("ble,bld->ed", context, d_attn, preferred_element_type=jnp.float32)
    d_context = split_heads(
        jnp.einsum("bld,ed->ble", d_attn, attn_out, preferred_element_type=jnp.float32).astype(
            jnp.bfloat16
        )
    )
    visible = key_visible(lengths, length)
    scores = head_scores(queries, key_rows, visible)
    probs_float = jnp.exp(scores - log_total)
    d_probs = jnp.einsum("bqhe,bkhe->bhqk", d_context, values, preferred_element_type=jnp.float32)
    d_values = jnp.einsum(
        "bhqk,bqhe->bkhe",
        probs_float.astype(jnp.bfloat16),
        d_context,
        preferred_element_type=jnp.float32,
    ).astype(jnp.bfloat16)
    d_scores = (
        probs_float * (d_probs - jnp.sum(probs_float * d_probs, axis=-1, keepdims=True))
    ).astype(jnp.bfloat16)
    d_queries = (
        jnp.einsum("bhqk,bkhe->bqhe", d_scores, key_rows, preferred_element_type=jnp.float32)
        * HD ** (-0.5)
    ).astype(jnp.bfloat16)
    d_keys = (
        jnp.einsum("bhqk,bqhe->bkhe", d_scores, queries, preferred_element_type=jnp.float32)
        * HD ** (-0.5)
    ).astype(jnp.bfloat16)
    query_grad = join_heads(d_queries)
    value_grad = join_heads(d_values)
    d_projected = jnp.stack([query_grad, join_heads(d_keys), value_grad], axis=2)
    grad_attn_in = jnp.einsum(
        "bld,blce->dce", tokens, d_projected, preferred_element_type=jnp.float32
    )
    token_part = jnp.einsum(
        "blce,dce->bld", d_projected, attn_in, preferred_element_type=jnp.float32
    )
    d_tokens = (
        d_first + lax.psum(token_part.astype(jnp.bfloat16), "tensor").astype(jnp.float32)
    ).astype(jnp.bfloat16)
    grad_in_bias = jnp.stack(
        [
            jnp.sum(query_grad.astype(jnp.float32), axis=(0, 1)),
            jnp.sum(value_grad.astype(jnp.float32), axis=(0, 1)),
        ]
    )
    grad_ffn_bias = jnp.sum(d_up.astype(jnp.float32), axis=(0, 1))
    grad_out_biases = jnp.stack(
        [
            jnp.sum(d_attn.astype(jnp.float32), axis=(0, 1)),
            jnp.sum(d_down.astype(jnp.float32), axis=(0, 1)),
        ]
    )
    grad_gains = jnp.stack([gain_first, gain_second])
    grad_shifts = jnp.stack([shift_first, shift_second])
    return (
        d_tokens,
        (
            grad_attn_in,
            grad_in_bias,
            grad_attn_out,
            grad_ffn_in,
            grad_ffn_bias,
            grad_ffn_out,
            grad_out_biases,
            grad_gains,
            grad_shifts,
        ),
    )


def contrastive(question_rows, passage_rows, own_positive, dataset_ids):
    class_scores = jnp.einsum(
        "gd,jd->gj", question_rows, passage_rows, preferred_element_type=jnp.float32
    ) * (score_gain * D ** (-0.5))
    columns = jnp.arange(passage_rows.shape[0], dtype=jnp.int32)
    chosen = own_positive[:, None] == columns[None, :]
    own_set = jnp.sum(jnp.where(chosen, dataset_ids[None, :], 0), axis=1)
    logits = jnp.where(dataset_ids[None, :] == own_set[:, None], class_scores, NEGATIVE)
    row_top = jnp.max(logits, axis=1, keepdims=True)
    log_total = row_top + jnp.log(jnp.sum(jnp.exp(logits - row_top), axis=1, keepdims=True))
    target = jnp.sum(jnp.where(chosen, class_scores, 0.0), axis=1)
    d_class = (jnp.exp(logits - log_total) - chosen.astype(jnp.float32)) * (
        score_gain * D ** (-0.5)
    )
    return (log_total[:, 0] - target, d_class)


def per_device(
    question_tokens,
    passage_tokens,
    question_cotangent,
    passage_cotangent,
    question_lengths,
    passage_lengths,
    dataset_ids,
    positives,
    attn_in,
    attn_in_bias,
    attn_out,
    ffn_in,
    ffn_in_bias,
    ffn_out,
    out_biases,
    norm_gains,
    norm_shifts,
):

    def encoder_params(encoder):
        return (
            attn_in[encoder],
            attn_in_bias[encoder],
            attn_out[encoder],
            ffn_in[encoder],
            ffn_in_bias[encoder],
            ffn_out[encoder],
            out_biases[encoder],
            norm_gains[encoder],
            norm_shifts[encoder],
        )

    question_params = encoder_params(0)
    passage_params = encoder_params(1)
    question_float, question_saved = encoder_forward(
        question_tokens, question_lengths, question_params
    )
    passage_float, passage_saved = encoder_forward(passage_tokens, passage_lengths, passage_params)
    question_heads = question_float[:, 0].astype(jnp.bfloat16)
    passage_heads = passage_float[:, 0].astype(jnp.bfloat16)
    local_groups = question_heads.shape[0]
    own_start = lax.axis_index("dp") * local_groups
    all_passages = lax.all_gather(passage_heads, "dp", axis=0, tiled=True)
    own_positive = lax.dynamic_slice_in_dim(positives, own_start, local_groups)
    cross, d_class = contrastive(question_heads, all_passages, own_positive, dataset_ids)
    total = lax.psum(jnp.sum(cross), "dp")
    contrastive_loss = total / all_passages.shape[0]
    d_question_heads = jnp.einsum(
        "gj,jd->gd", d_class, all_passages.astype(jnp.float32), precision=HIGHEST
    )
    question_heads_float = question_heads.astype(jnp.float32)
    d_passage_heads = lax.psum_scatter(
        jnp.einsum("gj,gd->jd", d_class, question_heads_float, precision=HIGHEST),
        "dp",
        scatter_dimension=0,
        tiled=True,
    )
    d_question_out = question_cotangent.astype(jnp.float32).at[:, 0].add(d_question_heads)
    d_passage_out = passage_cotangent.astype(jnp.float32).at[:, 0].add(d_passage_heads)
    passage_grad, passage_weights = encoder_backward(
        d_passage_out, passage_saved, passage_lengths, passage_params
    )
    question_grad, question_weights = encoder_backward(
        d_question_out, question_saved, question_lengths, question_params
    )
    joined = (
        lax.psum_scatter(question_weights[0], "dp", scatter_dimension=0, tiled=True),
        lax.psum_scatter(question_weights[1], "dp", scatter_dimension=1, tiled=True),
        lax.psum_scatter(question_weights[2], "dp", scatter_dimension=1, tiled=True),
        lax.psum_scatter(question_weights[3], "dp", scatter_dimension=0, tiled=True),
        lax.psum_scatter(question_weights[4], "dp", scatter_dimension=0, tiled=True),
        lax.psum_scatter(question_weights[5], "dp", scatter_dimension=1, tiled=True),
        lax.psum_scatter(question_weights[6], "dp", scatter_dimension=1, tiled=True),
        lax.psum_scatter(question_weights[7], "dp", scatter_dimension=1, tiled=True),
        lax.psum_scatter(question_weights[8], "dp", scatter_dimension=1, tiled=True),
        lax.psum_scatter(passage_weights[0], "dp", scatter_dimension=0, tiled=True),
        lax.psum_scatter(passage_weights[1], "dp", scatter_dimension=1, tiled=True),
        lax.psum_scatter(passage_weights[2], "dp", scatter_dimension=1, tiled=True),
        lax.psum_scatter(passage_weights[3], "dp", scatter_dimension=0, tiled=True),
        lax.psum_scatter(passage_weights[4], "dp", scatter_dimension=0, tiled=True),
        lax.psum_scatter(passage_weights[5], "dp", scatter_dimension=1, tiled=True),
        lax.psum_scatter(passage_weights[6], "dp", scatter_dimension=1, tiled=True),
        lax.psum_scatter(passage_weights[7], "dp", scatter_dimension=1, tiled=True),
        lax.psum_scatter(passage_weights[8], "dp", scatter_dimension=1, tiled=True),
    )
    question_parts = joined[:9]
    passage_parts = joined[9:]
    stacked = [
        jnp.stack([question_piece, passage_piece])
        for question_piece, passage_piece in zip(question_parts, passage_parts)
    ]
    return (
        question_float.astype(jnp.bfloat16),
        passage_float.astype(jnp.bfloat16),
        contrastive_loss,
        question_grad,
        passage_grad,
        stacked[0],
        stacked[1],
        stacked[2],
        stacked[3],
        stacked[4],
        stacked[5],
        stacked[6],
        stacked[7],
        stacked[8],
    )


def solution(mesh):
    in_specs = (
        P("dp", None, None),
        P("dp", None, None),
        P("dp", None, None),
        P("dp", None, None),
        P("dp"),
        P("dp"),
        P(),
        P(),
        P(None, None, None, "tensor"),
        P(None, None, "tensor"),
        P(None, "tensor", None),
        P(None, None, "tensor"),
        P(None, "tensor"),
        P(None, "tensor", None),
        P(),
        P(),
        P(),
    )
    out_specs = (
        P("dp", None, None),
        P("dp", None, None),
        P(),
        P("dp", None, None),
        P("dp", None, None),
        P(None, "dp", None, "tensor"),
        P(None, None, ("tensor", "dp")),
        P(None, "tensor", "dp"),
        P(None, "dp", "tensor"),
        P(None, ("tensor", "dp")),
        P(None, "tensor", "dp"),
        P(None, None, "dp"),
        P(None, None, "dp"),
        P(None, None, "dp"),
    )
    return jax.shard_map(
        per_device, mesh=mesh, in_specs=in_specs, out_specs=out_specs, check_vma=False
    )
```

profile of v0, /device:TPU:0, one launch (start us, length us, event | category | flops | bytes accessed | tf_op | source)
XLA Modules:
  0.0 2240.4 jit_solution(10756419954289291537)
XLA Ops:
  9.4 2.7 fusion.30
  21.1 2.1 fusion.6
  35.9 16.6 all-reduce.30.cloned.1.call-done
  59.6 2.4 fusion.97
  62.0 2.7 multiply_convert_fusion.2
  64.8 3.0 fusion.65
  68.3 2.1 fusion.82
  70.5 8.1 multiply_convert_fusion.1
  79.7 2.3 fusion.44
  83.8 2.4 convert_element_type.365
  90.7 12.3 all-reduce.28.cloned.1.call-done
  111.4 54.1 %all-gather = bf16[32,1,768]{2,1,0:T(2,128)(2,1)S(1)} all-gather(bf16[2,1,768]{2,1,0:T(2,128)(2,1)S(1)} %slice.261), channel_id=2, replica_groups=mesh['dp'=16,'tensor'=2] {'dp'}, dimensions={0}, use_global_device_ids=true | all-gather | bytes 52224 | tf_op jit(solution)/shard_map/all_gather | solution.py:295
  176.6 3.7 convert_reduce_fusion.3
  181.0 3.2 fusion.62
  184.2 89.4 %all-reduce.20.cloned.1.call-done = f32[32,768]{1,0:T(8,128)} async-done(((f32[32,768]{1,0:T(8,128)}), f32[32,768]{1,0:T(8,128)}) %all-reduce.20.cloned.1.call-update) | async-done | bytes 98320
  277.2 3.5 multiply_reduce_fusion.1
  283.1 5.8 convert_reduce_fusion
  290.0 2.3 fusion.41
  297.5 14.6 all-reduce.26.cloned.1.call-done
  312.1 2.2 multiply_reduce_fusion.10
  314.3 2.1 convert_reduce_fusion.7
  322.5 2.4 convert_reduce_fusion.8
  325.0 2.5 convert_reduce_fusion.9
  336.2 2.9 convert_reduce_fusion.4
  351.9 3.7 bitcast_convert_fusion
  360.5 4.0 convolution_bitcast_fusion.5
  364.5 6.3 copy.138
  370.9 2.4 convolution_bitcast_fusion.4
  373.3 6.3 copy.136
  380.8 3.0 convolution_bitcast_fusion.1
  385.2 5.1 convolution_bitcast_fusion
  391.4 3.0 convolution_bitcast_fusion.3
  395.4 5.0 convolution_bitcast_fusion.2
  402.8 77.1 %all-reduce.7 = (f32[]{:T(128)}, f32[2,384]{1,0:T(2,128)S(1)}, f32[2,384]{1,0:T(2,128)S(1)}, f32[1536]{0:T(1024)S(1)}, f32[1536]{0:T(1024)S(1)}) all-reduce(f32[]{:T(128)} %get-tuple-element.125, f32[2,384]{1,0:T(2,128)S(1)} %pad_maximum_fusion.17, f32[2,384]{1,0:T(2,128)S(1)} %pad_maximum_fusion.16, ...), channel_id=1, replica_groups=mesh['dp'=16,'tensor'=2] {'dp'}, use_global_device_ids=true, to_apply=%region_21.22 | all-reduce | flops 4609 | bytes 36872 | tf_op jit(solution)/shard_map/psum | solution.py:298
  482.9 109.3 %reduce-scatter.49.cloned.1.call-done = f32[48,2]{1,0:T(8,128)} async-done(((f32[768,2]{1,0:T(8,128)}), f32[48,2]{1,0:T(8,128)}) %reduce-scatter.49.cloned.1.call-update) | async-done | bytes 400
  593.0 125.3 %reduce-scatter.45.cloned.1.call-done = f32[48,2]{1,0:T(8,128)} async-done(((f32[768,2]{1,0:T(8,128)}), f32[48,2]{1,0:T(8,128)}) %reduce-scatter.45.cloned.1.call-update) | async-done | bytes 400
  719.0 124.5 %reduce-scatter.39.cloned.1.call-done = f32[48,2]{1,0:T(8,128)} async-done(((f32[768,2]{1,0:T(8,128)}), f32[48,2]{1,0:T(8,128)}) %reduce-scatter.39.cloned.1.call-update) | async-done | bytes 400
  844.3 125.3 %reduce-scatter.47.cloned.1.call-done = f32[48,2]{1,0:T(8,128)} async-done(((f32[768,2]{1,0:T(8,128)}), f32[48,2]{1,0:T(8,128)}) %reduce-scatter.47.cloned.1.call-update) | async-done | bytes 400
  970.4 124.4 %reduce-scatter.43.cloned.1.call-done = f32[48,2]{1,0:T(8,128)} async-done(((f32[768,2]{1,0:T(8,128)}), f32[48,2]{1,0:T(8,128)}) %reduce-scatter.43.cloned.1.call-update) | async-done | bytes 400
  1097.3 19.3 all-reduce.24.cloned.1.call-done
  1118.2 2.2 add_convert_fusion.1
  1120.4 126.5 %reduce-scatter.29.cloned.1.call-done = f32[384,48]{0,1:T(8,128)} async-done(((f32[384,768]{0,1:T(8,128)}), f32[384,48]{0,1:T(8,128)}) %reduce-scatter.29.cloned.1.call-update) | async-done | bytes 73744 | tf_op jit(solution)/shard_map/reduce_scatter | solution.py:330
  1246.9 128.2 %reduce-scatter.27.cloned.1.call-done = f32[384,48]{0,1:T(8,128)} async-done(((f32[384,768]{0,1:T(8,128)}), f32[384,48]{0,1:T(8,128)}) %reduce-scatter.27.cloned.1.call-update) | async-done | bytes 73744 | tf_op jit(solution)/shard_map/reduce_scatter | solution.py:321
  1376.7 285.1 %all-reduce.22.cloned.1.call-done = (f32[768,3,384]{2,1,0:T(4,128)}, f32[768,3,384]{2,1,0:T(4,128)}) async-done(((f32[768,3,384]{2,1,0:T(4,128)}, f32[768,3,384]{2,1,0:T(4,128)}), (f32[768,3,384]{2,1,0:T(4,128)}, f32[768,3,384]{2,1,0:T(4,128)})) %all-reduce.22.cloned.1.call-update) | async-done | bytes 7077904
  1664.7 138.8 %reduce-scatter.35.cloned.1.call-done = f32[1536,48]{0,1:T(8,128)} async-done(((f32[1536,768]{0,1:T(8,128)}), f32[1536,48]{0,1:T(8,128)}) %reduce-scatter.35.cloned.1.call-update) | async-done | bytes 294928 | tf_op jit(solution)/shard_map/reduce_scatter | solution.py:324
  1803.5 142.4 %reduce-scatter.37.cloned.1.call-done = f32[1536,48]{0,1:T(8,128)} async-done(((f32[1536,768]{0,1:T(8,128)}), f32[1536,48]{0,1:T(8,128)}) %reduce-scatter.37.cloned.1.call-update) | async-done | bytes 294928 | tf_op jit(solution)/shard_map/reduce_scatter | solution.py:333
  1947.8 139.9 %reduce-scatter.31.cloned.1.call-done = f32[48,1536]{1,0:T(8,128)} async-done(((f32[768,1536]{1,0:T(8,128)}), f32[48,1536]{1,0:T(8,128)}) %reduce-scatter.31.cloned.1.call-update) | async-done | bytes 294928 | tf_op jit(solution)/shard_map/reduce_scatter | solution.py:322
  2087.7 142.6 %reduce-scatter.33.cloned.1.call-done = f32[48,1536]{1,0:T(8,128)} async-done(((f32[768,1536]{1,0:T(8,128)}), f32[48,1536]{1,0:T(8,128)}) %reduce-scatter.33.cloned.1.call-update) | async-done | bytes 294928 | tf_op jit(solution)/shard_map/reduce_scatter | solution.py:331
  (466 shorter events, 125.0 us)
Async XLA Ops:
  7.2 45.3 %all-reduce.30.cloned.1.call-start = ((), (), s32[]{:S(2)}) async-start(), calls=%async_computation.29 | async-start | bytes 1966080 | tf_op jit(solution)/shard_map/psum | solution.py:86
  13.5 7.6 copy-start.80
  13.6 13.3 copy-start.88
  30.0 72.9 %all-reduce.28.cloned.1.call-start = ((), (), s32[]{:S(2)}) async-start(), calls=%async_computation.28 | async-start | bytes 1966080 | tf_op jit(solution)/shard_map/psum | solution.py:99
  52.5 7.1 copy-start.115
  54.9 13.3 slice-start.2
  56.8 10.9 copy-start.76
  58.7 9.1 copy-start.82
  59.6 8.7 slice-start.3
  67.8 12.0 slice-start
  68.3 11.4 slice-start.1
  70.5 8.1 copy-start.35
  82.0 191.6 %all-reduce.20.cloned.1.call-start = ((), (), s32[]{:S(2)}) async-start(), calls=%async_computation.24 | async-start | bytes 196608
  103.0 7.1 copy-start.1
  103.0 7.1 copy-start.12
  103.0 7.1 copy-start.65
  103.0 7.1 copy-start.73
  103.0 7.1 copy-start.91
  105.5 60.0 %copy-start.121 = (s32[32]{0:T(128)S(1)}, s32[32]{0:T(128)}, u32[]{:S(2)}) copy-start(s32[32]{0:T(128)} %param.27) | copy-start | bytes 388
  105.6 59.9 %copy-start.123 = (s32[2]{0:T(128)S(1)}, s32[2]{0:T(128)}, u32[]{:S(2)}) copy-start(s32[2]{0:T(128)} %copy-done.122) | copy-start | bytes 28
  105.6 59.9 %copy-start.124 = (s32[2]{0:T(128)S(1)}, s32[2]{0:T(128)}, u32[]{:S(2)}) copy-start(s32[2]{0:T(128)} %select_reduce_fusion.1) | copy-start | bytes 28
  107.3 60.1 %copy-start.78 = (f32[2,256]{1,0:T(2,128)}, f32[2,256]{1,0:T(2,128)S(1)}, u32[]{:S(2)}) copy-start(f32[2,256]{1,0:T(2,128)S(1)} %broadcast_multiply_fusion.4) | copy-start | bytes 6148
  109.2 58.3 %copy-start.84 = (f32[2,256]{1,0:T(2,128)}, f32[2,256]{1,0:T(2,128)S(1)}, u32[]{:S(2)}) copy-start(f32[2,256]{1,0:T(2,128)S(1)} %add_rsqrt_fusion) | copy-start | bytes 6148
  174.4 137.7 %all-reduce.26.cloned.1.call-start = ((), (), s32[]{:S(2)}) async-start(), calls=%async_computation.27 | async-start | bytes 1966080 | tf_op jit(solution)/shard_map/psum | solution.py:160
  280.7 9.3 slice-start.4
  281.4 7.5 copy-start.15
  283.1 7.0 slice-start.5
  292.3 189.7 %reduce-scatter.41.cloned.1.call-start = ((), (), s32[]{:S(2)}) async-start(), calls=%async_computation.19 | async-start | bytes 417792
  316.4 12.9 copy-start.71
  321.0 8.3 copy-start.8
  321.0 8.3 copy-start.11
  321.0 8.3 copy-start.16
  321.0 8.3 copy-start.37
  321.0 8.3 copy-start.77
  321.0 8.3 copy-start.83
  344.0 248.2 %reduce-scatter.49.cloned.1.call-start = ((), (), s32[]{:S(2)}) async-start(), calls=%async_computation.23 | async-start | bytes 417792
  345.0 373.2 %reduce-scatter.45.cloned.1.call-start = ((), (), s32[]{:S(2)}) async-start(), calls=%async_computation.21 | async-start | bytes 417792
  346.1 497.4 %reduce-scatter.39.cloned.1.call-start = ((), (), s32[]{:S(2)}) async-start(), calls=%async_computation.18 | async-start | bytes 417792
  347.2 622.4 %reduce-scatter.47.cloned.1.call-start = ((), (), s32[]{:S(2)}) async-start(), calls=%async_computation.22 | async-start | bytes 417792
  348.3 746.5 %reduce-scatter.43.cloned.1.call-start = ((), (), s32[]{:S(2)}) async-start(), calls=%async_computation.20 | async-start | bytes 417792
  351.1 765.5 %all-reduce.24.cloned.1.call-start = ((), (), s32[]{:S(2)}) async-start(), calls=%async_computation.26 | async-start | bytes 1966080 | tf_op jit(solution)/shard_map/psum | solution.py:202
  357.0 889.9 %reduce-scatter.29.cloned.1.call-start = ((), (), s32[]{:S(2)}) async-start(), calls=%async_computation.13 | async-start | bytes 1253376 | tf_op jit(solution)/shard_map/reduce_scatter | solution.py:330
  358.9 1016.2 %reduce-scatter.27.cloned.1.call-start = ((), (), s32[]{:S(2)}) async-start(), calls=%async_computation.12 | async-start | bytes 1253376 | tf_op jit(solution)/shard_map/reduce_scatter | solution.py:321
  360.4 1301.4 %all-reduce.22.cloned.1.call-start = ((), (), s32[]{:S(2)}) async-start(), calls=%async_computation.25 | async-start | bytes 18874368
  379.7 1423.9 %reduce-scatter.35.cloned.1.call-start = ((), (), s32[]{:S(2)}) async-start(), calls=%async_computation.16 | async-start | bytes 5013504 | tf_op jit(solution)/shard_map/reduce_scatter | solution.py:324
  383.8 1562.2 %reduce-scatter.37.cloned.1.call-start = ((), (), s32[]{:S(2)}) async-start(), calls=%async_computation.17 | async-start | bytes 5013504 | tf_op jit(solution)/shard_map/reduce_scatter | solution.py:333
  390.3 1697.4 %reduce-scatter.31.cloned.1.call-start = ((), (), s32[]{:S(2)}) async-start(), calls=%async_computation.14 | async-start | bytes 5013504 | tf_op jit(solution)/shard_map/reduce_scatter | solution.py:322
  394.3 1836.0 %reduce-scatter.33.cloned.1.call-start = ((), (), s32[]{:S(2)}) async-start(), calls=%async_computation.15 | async-start | bytes 5013504 | tf_op jit(solution)/shard_map/reduce_scatter | solution.py:331
  (101 other events, 319.9 us)
Sparse Core Ops, SparseCore 0:
  30.2 22.2 all-reduce.29
  82.1 20.7 all-reduce.27
  174.5 99.0 all-reduce.19
  292.5 19.5 all-reduce.25
  344.1 122.8 reduce-scatter.40
  471.5 120.6 reduce-scatter.48
  597.5 120.6 reduce-scatter.44
  722.9 120.5 reduce-scatter.38
  848.9 120.6 reduce-scatter.46
  974.1 120.6 reduce-scatter.42
  1097.9 18.6 all-reduce.23
  1121.2 125.6 reduce-scatter.28
  1251.7 123.4 reduce-scatter.26
  1381.3 280.4 all-reduce.21
  1666.8 136.6 reduce-scatter.34
  1809.4 136.4 reduce-scatter.36
  1950.9 136.7 reduce-scatter.30
  2093.6 136.6 reduce-scatter.32
where the time goes:
time: 2240 us
  waiting for transfers between devices  1860 us (83%)
  blocking collectives  131 us (6%)
  matrix products  86.1 us (4%)
  other arithmetic  69.3 us (3%)
  local copies, waits for them, and re-layouts  67.4 us (3%)
    unnamed x26, waiting for transfers between devices  983 us
    reduce_scatter x1, waiting for transfers between devices, per_device(): lax.psum_scatter(passage_weights[3], 'dp', scatter_dimension=0, tiled=True)  143 us
    reduce_scatter x1, waiting for transfers between devices, per_device(): lax.psum_scatter(passage_weights[5], 'dp', scatter_dimension=1, tiled=True)  142 us
    reduce_scatter x1, waiting for transfers between devices, per_device(): lax.psum_scatter(question_weights[3], 'dp', scatter_dimension=0, tiled=True)  140 us
    reduce_scatter x1, waiting for transfers between devices, per_device(): lax.psum_scatter(question_weights[5], 'dp', scatter_dimension=1, tiled=True)  139 us
    reduce_scatter x1, waiting for transfers between devices, per_device(): lax.psum_scatter(question_weights[2], 'dp', scatter_dimension=1, tiled=True)  128 us
    reduce_scatter x1, waiting for transfers between devices, per_device(): lax.psum_scatter(passage_weights[2], 'dp', scatter_dimension=1, tiled=True)  127 us
    psum x1, blocking collectives, per_device(): total = lax.psum(jnp.sum(cross), 'dp')  77.1 us
  transfers between devices with their start and end apart: 18, of which 17 were waited for; matrix products, arithmetic and copies ran while one was open for 4% of the time, Pallas kernels for 0%

commit v1 on v0

--- a/solution.py
+++ b/solution.py
@@ -3,6 +3,8 @@
 import jax
 import jax.numpy as jnp
 from jax import lax
+from jax.experimental import pallas as pl
+from jax.experimental.pallas import tpu as pltpu
 from jax.sharding import PartitionSpec as P
 
 D = 768
@@ -359,6 +361,856 @@
     )
 
 
+MESH_ID = pl.DeviceIdType.MESH
+F32 = jnp.float32
+BF16 = jnp.bfloat16
+ZN = 4
+ROWS_OUT = 48
+JOBS = 12
+COLS = 384
+D1, DZ, D3, DS = 8, 4, 2, 2
+TOKS = (128, 512)
+BLK = (128, 256)
+SMALL = 24
+
+
+def dot(a, b):
+    return jnp.dot(a, b, preferred_element_type=F32)
+
+
+def dot_t(a, b):
+    return lax.dot_general(a, b, (((1,), (1,)), ((), ())), preferred_element_type=F32)
+
+
+def t_dot(a, b):
+    return lax.dot_general(a, b, (((0,), (0,)), ((), ())), preferred_element_type=F32)
+
+
+def gelu_and_slope(u):
+    size = jnp.abs(u)
+    bell = jnp.exp(-0.5 * u * u)
+    t = 1.0 / (1.0 + (0.3275911 * 0.7071067811865476) * size)
+    poly = t * (
+        0.127414796
+        + t * (-0.142248368 + t * (0.7107068705 + t * (-0.7265760135 + t * 0.5307027145)))
+    )
+    tail = poly * bell
+    phi = jnp.where(u >= 0.0, 1.0 - tail, tail)
+    return u * phi, phi + u * bell * 0.3989422804014327
+
+
+def row_mean(v):
+    return jnp.sum(v, axis=-1, keepdims=True) * (1.0 / D)
+
+
+def fold8(v):
+    return jnp.sum(v.reshape(v.shape[0] // 8, 8, v.shape[1]), axis=0)
+
+
+def rows_at(start, size, step=16):
+    return pl.ds(pl.multiple_of(start, step), size)
+
+
+def fused_kernel(
+    xq_in, xp_in, cq_in, cp_in, qlen, plen, dsid, posi,
+    win_in, bin_in, wo_in, wf_in, bfi_in, wd_in, bo_in, gain_in, shift_in,
+    oq_out, op_out, loss_out, gq_out, gp_out, g_in, g_out, g_fi, g_fo, sm_out,
+    win, wo, wf, wd, xq, xp, cq, cp, qkvq, qkvp, prq, prp, hq, hp, n1q, n1p, n2q, n2p,
+    i1q, i1p, i2q, i2p, sq, sp, obq, obp, ddq, ddp, dcq, dcp, ballq, ballp, atq, atp,
+    exsq, exsp, exrq, exrp, par, pin, pfi, masks, hg, hf, dh, acc_s, acc_b, acc_f, smb, smr,
+    p1s, p1r, zr, zl, p3r,
+    in_sem, out_sem, exs_sem, exr_sem, hgs_sem, hgr_sem, sms_sem, smr_sem,
+    p1s_sem, p1r_sem, zrs_sem, zrr_sem, zls_sem, zlr_sem, p3s_sem, p3r_sem,
+    *, last,
+):
+    me = lax.axis_index("dp")
+    core = lax.axis_index("tensor")
+    z, y, x = me // 4, (me // 2) % 2, me % 2
+    partner = {"dp": me, "tensor": 1 - core}
+    at_x = {"dp": me + 1 - 2 * x, "tensor": core}
+    at_y = {"dp": me + 2 - 4 * y, "tensor": core}
+
+    def at_dp(index):
+        return {"dp": index, "tensor": core}
+
+    X, COT, QKV, PR, HID = (xq, xp), (cq, cp), (qkvq, qkvp), (prq, prp), (hq, hp)
+    N1, N2, I1, I2, SLOPE = (n1q, n1p), (n2q, n2p), (i1q, i1p), (i2q, i2p), (sq, sp)
+    OB, DD, DC, BALL, AT = (obq, obp), (ddq, ddp), (dcq, dcp), (ballq, ballp), (atq, atp)
+    EXS, EXR = (exsq, exsp), (exrq, exrp)
+
+    loads = [
+        (xq_in, xq),
+        *[(win_in.at[0, j], win.at[0, :, pl.ds(j * COLS, COLS)]) for j in range(3)],
+        (xp_in, xp),
+        *[(win_in.at[1, j], win.at[1, :, pl.ds(j * COLS, COLS)]) for j in range(3)],
+        (wo_in.at[0], wo.at[0]),
+        (wo_in.at[1], wo.at[1]),
+        (wf_in.at[0], wf.at[0]),
+        (wf_in.at[1], wf.at[1]),
+        (wd_in.at[0], wd.at[0]),
+        (wd_in.at[1], wd.at[1]),
+        (cq_in, cq),
+        (cp_in, cp),
+    ]
+    loads = [pltpu.make_async_copy(s, d, in_sem.at[i]) for i, (s, d) in enumerate(loads)]
+    for copy in loads:
+        copy.start()
+    ready = set()
+
+    def need(*which):
+        for i in which:
+            if i not in ready:
+                loads[i].wait()
+                ready.add(i)
+
+    barrier = pltpu.get_barrier_semaphore()
+    pl.semaphore_signal(barrier, inc=1, device_id=partner, device_id_type=MESH_ID)
+    for k in range(1, 16):
+        pl.semaphore_signal(barrier, inc=1, device_id=at_dp(me ^ k), device_id_type=MESH_ID)
+
+    for e in range(2):
+        for i in range(2):
+            par[e * 8 + i : e * 8 + i + 1, :] = bo_in[e].astype(F32)[i : i + 1]
+            par[e * 8 + 2 + i : e * 8 + 3 + i, :] = gain_in[e].astype(F32)[i : i + 1]
+            par[e * 8 + 4 + i : e * 8 + 5 + i, :] = shift_in[e].astype(F32)[i : i + 1]
+            pin[e * 2 + i : e * 2 + i + 1, :] = bin_in[e].astype(F32)[i : i + 1]
+        pfi[e : e + 1, :] = bfi_in[...].astype(F32)[e : e + 1]
+    acc_s[...] = jnp.zeros_like(acc_s)
+    acc_b[...] = jnp.zeros_like(acc_b)
+    acc_f[...] = jnp.zeros_like(acc_f)
+
+    r32 = lax.broadcasted_iota(jnp.int32, (32, 32), 0)
+    c32 = lax.broadcasted_iota(jnp.int32, (32, 32), 1)
+    own_pos = jnp.zeros((32, 32), F32)
+    set_col = jnp.zeros((32, 32), F32)
+    for g in range(32):
+        at = (g % 2) * 16 + g // 2
+        own_pos = jnp.where(r32 == at, posi[g].astype(F32), own_pos)
+        set_col = jnp.where(c32 == at, dsid[g].astype(F32), set_col)
+    col_group = ((c32 % 16) * 2 + c32 // 16).astype(F32)
+    chosen = jnp.where(own_pos == col_group, 1.0, 0.0)
+    own_set = jnp.sum(chosen * set_col, axis=1, keepdims=True)
+    masks[0:32, :] = chosen
+    masks[32:64, :] = jnp.where(set_col == own_set, 1.0, 0.0)
+
+    lane_lo = lax.broadcasted_iota(jnp.int32, (1, 128), 1) < HD
+
+    def side(v, hh):
+        return jnp.where(lane_lo if hh == 0 else jnp.logical_not(lane_lo), v, jnp.zeros_like(v))
+
+    def exchange(e, b, parity):
+        slot = 0 if e == 0 else 1 + b
+        rows = rows_at(b * BLK[e], BLK[e]) if not isinstance(b, int) else pl.ds(b * BLK[e], BLK[e])
+        return pltpu.make_async_remote_copy(
+            src_ref=EXS[e].at[rows],
+            dst_ref=EXR[e].at[parity, rows],
+            send_sem=exs_sem.at[slot],
+            recv_sem=exr_sem.at[parity, slot],
+            device_id=partner,
+            device_id_type=MESH_ID,
+        )
+
+    def block_rows(e, b):
+        if e == 0:
+            return pl.ds(0, BLK[0])
+        return rows_at(b * BLK[1], BLK[1], BLK[1])
+
+    def blocks(e, body):
+        if e == 0:
+            body(0)
+        else:
+            pl.loop(0, 2)(body)
+
+    def attend(e, b):
+        size = BLK[e]
+        rows = block_rows(e, b)
+        xb = X[e][rows, :]
+        for j in range(3):
+            cols = pl.ds(j * COLS, COLS)
+            got = dot(xb, win[e, :, cols])
+            if j == 0:
+                got = (got + pin[e * 2 : e * 2 + 1, :]).astype(BF16) * jnp.asarray(HD**-0.5, BF16)
+            elif j == 2:
+                got = got + pin[e * 2 + 1 : e * 2 + 2, :]
+            QKV[e][rows, cols] = got.astype(BF16)
+
+        col = lax.broadcasted_iota(jnp.int32, (size, size), 1)
+        if e == 0:
+            row = lax.broadcasted_iota(jnp.int32, (size, size), 0)
+            first = jnp.logical_and(row < 64, col < qlen[0])
+            second = jnp.logical_and(
+                row >= 64, jnp.logical_and(col >= 64, col < 64 + qlen[1])
+            )
+            seen = jnp.logical_or(first, second)
+        else:
+            seen = col < plen[b]
+
+        @pl.loop(0, 3)
+        def _(pair):
+            q2 = QKV[e][rows, rows_at(pair * 128, 128, 128)]
+            k2 = QKV[e][rows, rows_at(COLS + pair * 128, 128, 128)]
+            v2 = QKV[e][rows, rows_at(2 * COLS + pair * 128, 128, 128)]
+            total = jnp.zeros((size, 128), F32)
+            for hh in range(2):
+                s = dot_t(side(q2, hh), k2)
+                s = jnp.where(seen, s, NEGATIVE)
+                p = jnp.exp(s - jnp.max(s, axis=-1, keepdims=True))
+                p = (p * (1.0 / jnp.sum(p, axis=-1, keepdims=True))).astype(BF16)
+                PR[e][b, pair * 2 + hh] = p
+                total = total + dot(p, side(v2, hh))
+            BALL[e][rows, rows_at(8 * COLS + pair * 128, 128, 128)] = total.astype(BF16)
+
+        ctx = BALL[e][rows, pl.ds(8 * COLS, COLS)]
+        EXS[e][rows, :] = dot(ctx, wo[e]).astype(BF16)
+        exchange(e, b, 0).start()
+
+    CH = 32
+
+    def first_norm(e, b):
+        exchange(e, b, 0).wait()
+
+        @pl.loop(0, BLK[e] // CH)
+        def _(c):
+            rows = rows_at(b * BLK[e] + c * CH, CH, CH)
+            v = (
+                X[e][rows, :].astype(F32)
+                + (EXS[e][rows, :].astype(F32) + EXR[e][0, rows, :].astype(F32))
+                + par[e * 8 : e * 8 + 1, :]
+            )
+            v = v - row_mean(v)
+            inv = lax.rsqrt(row_mean(v * v) + EPSILON)
+            n = v * inv
+            N1[e][rows, :] = n
+            I1[e][rows, :] = inv
+            HID[e][rows, :] = (
+                n * par[e * 8 + 2 : e * 8 + 3, :] + par[e * 8 + 4 : e * 8 + 5, :]
+            ).astype(BF16)
+
+    def feed(e, b):
+        rows = block_rows(e, b)
+
+        @pl.loop(0, 6)
+        def _(n):
+            cols = rows_at(n * 256, 256, 256)
+            u = dot(HID[e][rows, :], wf[e, :, cols]) + pfi[e : e + 1, cols]
+            a, slope = gelu_and_slope(u)
+            BALL[e][rows, cols] = a.astype(BF16)
+            SLOPE[e][rows, cols] = slope.astype(BF16)
+
+        @pl.loop(0, 3)
+        def _(n):
+            cols = rows_at(n * 256, 256, 256)
+            EXS[e][rows, cols] = dot(BALL[e][rows, pl.ds(0, FF_HERE)], wd[e, :, cols]).astype(BF16)
+
+        exchange(e, b, 1).start()
+
+    def second_norm(e, b):
+        exchange(e, b, 1).wait()
+
+        @pl.loop(0, BLK[e] // CH)
+        def _(c):
+            rows = rows_at(b * BLK[e] + c * CH, CH, CH)
+            v = (
+                HID[e][rows, :].astype(F32)
+                + (EXS[e][rows, :].astype(F32) + EXR[e][1, rows, :].astype(F32))
+                + par[e * 8 + 1 : e * 8 + 2, :]
+            )
+            v = v - row_mean(v)
+            inv = lax.rsqrt(row_mean(v * v) + EPSILON)
+            n = v * inv
+            N2[e][rows, :] = n
+            I2[e][rows, :] = inv
+            OB[e][rows, :] = (
+                n * par[e * 8 + 3 : e * 8 + 4, :] + par[e * 8 + 5 : e * 8 + 6, :]
+            ).astype(BF16)
+
+    need(0, 1, 2, 3, 8)
+    pl.semaphore_wait(barrier, 16)
+    attend(0, 0)
+    need(4, 5, 6, 7, 9)
+    blocks(1, lambda b: attend(1, b))
+    first_norm(0, 0)
+    need(10, 12)
+    feed(0, 0)
+    need(11, 13)
+
+    def passage_mid(b):
+        first_norm(1, b)
+        feed(1, b)
+
+    blocks(1, passage_mid)
+    second_norm(0, 0)
+    blocks(1, lambda b: second_norm(1, b))
+    out_q = pltpu.make_async_copy(obq, oq_out, out_sem.at[0])
+    out_p = pltpu.make_async_copy(obp, op_out, out_sem.at[1])
+    out_q.start()
+    out_p.start()
+
+    pieces = []
+    for ref, at in ((obq, 0), (obq, 64), (obp, 0), (obp, 256)):
+        head = ref[at : at + 16, :].astype(F32)[0:1]
+        pieces += [head[:, k * 256 : (k + 1) * 256] for k in range(3)]
+    pieces.append(jnp.zeros((4, 256), F32))
+    hg[me] = jnp.concatenate(pieces, axis=0).astype(BF16)
+
+    def heads(k):
+        return pltpu.make_async_remote_copy(
+            src_ref=hg.at[me],
+            dst_ref=hg.at[me],
+            send_sem=hgs_sem.at[k],
+            recv_sem=hgr_sem.at[k],
+            device_id=at_dp(me ^ k),
+            device_id_type=MESH_ID,
+        )
+
+    for k in range(1, 16):
+        heads(k).start()
+    need(14, 15)
+    for k in range(1, 16):
+        copy = pltpu.make_async_remote_copy(
+            src_ref=hg.at[me],
+            dst_ref=hg.at[me ^ k],
+            send_sem=hgs_sem.at[k],
+            recv_sem=hgr_sem.at[k],
+            device_id=at_dp(me ^ k),
+            device_id_type=MESH_ID,
+        )
+        copy.wait()
+    gathered = hg[...].astype(F32).reshape(256, 256)
+    hf[0] = gathered[:, 0:128]
+    hf[1] = gathered[:, 128:256]
+
+    def all_heads(first):
+        groups = []
+        for i in range(2):
+            parts = [
+                hf[c, pl.ds(first + i * 3 + k, 16, stride=16), :] for k in range(3) for c in range(2)
+            ]
+            groups.append(jnp.concatenate(parts, axis=1))
+        return jnp.concatenate(groups, axis=0)
+
+    heads_q, heads_p = all_heads(0), all_heads(6)
+    gain = score_gain * D ** (-0.5)
+    class_scores = dot_t(heads_q.astype(BF16), heads_p.astype(BF16)) * gain
+    chosen = masks[0:32, :]
+    logits = jnp.where(masks[32:64, :] > 0.5, class_scores, NEGATIVE)
+    top = jnp.max(logits, axis=1, keepdims=True)
+    log_total = top + jnp.log(jnp.sum(jnp.exp(logits - top), axis=1, keepdims=True))
+    target = jnp.sum(chosen * class_scores, axis=1, keepdims=True)
+    loss = jnp.sum(log_total - target, axis=0, keepdims=True) * (1.0 / 32)
+    loss_out[...] = jnp.broadcast_to(loss, loss_out.shape)
+    d_class = (jnp.exp(logits - log_total) - chosen) * gain
+    dh[0:32, :] = lax.dot_general(
+        d_class, heads_p, (((1,), (0,)), ((), ())), precision=HIGHEST, preferred_element_type=F32
+    )
+    dh[32:64, :] = lax.dot_general(
+        d_class, heads_q, (((0,), (0,)), ((), ())), precision=HIGHEST, preferred_element_type=F32
+    )
+
+    def norm_back(incoming, n, inv, scale):
+        scaled = incoming * scale
+        return inv * (scaled - row_mean(scaled) - n * row_mean(scaled * n))
+
+    def transpose_into(e, k, src, b, width=D):
+        rows = block_rows(e, b)
+
+        @pl.loop(0, width // 256)
+        def _(c):
+            tile = src[rows, rows_at(c * 256, 256, 256)]
+            AT[e][rows_at(k * D + c * 256, 256, 256), rows] = tile.T
+
+    def second_back(e, b):
+        row0 = lax.broadcasted_iota(jnp.int32, (CH, 1), 0)
+        seqs = 2 if e == 0 else 1
+        length = 64 if e == 0 else 256
+        for i in range(seqs):
+            group = i if e == 0 else b
+            extra = dh[pl.ds(e * 32 + group * 16 + me, 1), :]
+
+            @pl.loop(0, length // CH)
+            def _(c):
+                rows = rows_at(group * length + c * CH, CH, CH)
+                add = jnp.where(row0 + c * CH == 0, extra, 0.0)
+                d = COT[e][rows, :].astype(F32) + add
+                n = N2[e][rows, :]
+                out = norm_back(d, n, I2[e][rows, :], par[e * 8 + 3 : e * 8 + 4, :])
+                N2[e][rows, :] = out
+                low = out.astype(BF16)
+                DD[e][rows, :] = low
+                acc_s[e * 6 + 1] += fold8(d * n)
+                acc_s[e * 6 + 3] += fold8(d)
+                acc_s[e * 6 + 5] += fold8(low.astype(F32))
+
+        transpose_into(e, 0, DD[e], b)
+
+    def feed_back(e, b):
+        rows = block_rows(e, b)
+
+        @pl.loop(0, 6)
+        def _(n):
+            cols = rows_at(n * 256, 256, 256)
+            d = dot_t(DD[e][rows, :], wd[e, cols, :]) * SLOPE[e][rows, cols].astype(F32)
+            d = d.astype(BF16)
+            BALL[e][rows, rows_at(4 * COLS + n * 256, 256, 256)] = d
+            acc_f[e, :, cols] += fold8(d.astype(F32))
+
+        @pl.loop(0, 3)
+        def _(n):
+            cols = rows_at(n * 256, 256, 256)
+            EXS[e][rows, cols] = dot_t(BALL[e][rows, pl.ds(4 * COLS, FF_HERE)], wf[e, cols, :]).astype(BF16)
+
+        exchange(e, b, 0).start()
+        transpose_into(e, 1, HID[e], b)
+
+    def first_back(e, b):
+        exchange(e, b, 0).wait()
+
+        @pl.loop(0, BLK[e] // CH)
+        def _(c):
+            rows = rows_at(b * BLK[e] + c * CH, CH, CH)
+            d = N2[e][rows, :] + (EXS[e][rows, :].astype(F32) + EXR[e][0, rows, :].astype(F32))
+            n = N1[e][rows, :]
+            out = norm_back(d, n, I1[e][rows, :], par[e * 8 + 2 : e * 8 + 3, :])
+            N1[e][rows, :] = out
+            low = out.astype(BF16)
+            DD[e][rows, :] = low
+            acc_s[e * 6 + 0] += fold8(d * n)
+            acc_s[e * 6 + 2] += fold8(d)
+            acc_s[e * 6 + 4] += fold8(low.astype(F32))
+
+        transpose_into(e, 2, DD[e], b)
+
+    def attend_back(e, b):
+        rows = block_rows(e, b)
+        size = BLK[e]
+        DC[e][rows, :] = dot_t(DD[e][rows, :], wo[e]).astype(BF16)
+
+        @pl.loop(0, 3)
+        def _(pair):
+            q2 = QKV[e][rows, rows_at(pair * 128, 128, 128)]
+            k2 = QKV[e][rows, rows_at(COLS + pair * 128, 128, 128)]
+            v2 = QKV[e][rows, rows_at(2 * COLS + pair * 128, 128, 128)]
+            dc2 = DC[e][rows, rows_at(pair * 128, 128, 128)]
+            dq = jnp.zeros((size, 128), F32)
+            dk = jnp.zeros((size, 128), F32)
+            dv = jnp.zeros((size, 128), F32)
+            for hh in range(2):
+                low = PR[e][b, pair * 2 + hh]
+                p = low.astype(F32)
+                dch = side(dc2, hh)
+                dp = dot_t(dch, v2)
+                ds = (p * (dp - jnp.sum(p * dp, axis=-1, keepdims=True))).astype(BF16)
+                dv = dv + t_dot(low, dch)
+                dq = dq + dot(ds, side(k2, hh))
+                dk = dk + t_dot(ds, side(q2, hh))
+            dq = (dq * HD**-0.5).astype(BF16)
+            dv = dv.astype(BF16)
+            cols = rows_at(pair * 128, 128, 128)
+            BALL[e][rows, rows_at(9 * COLS + pair * 128, 128, 128)] = dq
+            BALL[e][rows, rows_at(10 * COLS + pair * 128, 128, 128)] = dk.astype(BF16)
+            BALL[e][rows, rows_at(11 * COLS + pair * 128, 128, 128)] = dv
+            acc_b[e, :, cols] += fold8(dq.astype(F32))
+            acc_b[e, :, rows_at(COLS + pair * 128, 128, 128)] += fold8(dv.astype(F32))
+
+        transpose_into(e, 3, X[e], b)
+
+    def token_back(e, b):
+        rows = block_rows(e, b)
+
+        @pl.loop(0, 3)
+        def _(n):
+            cols = rows_at(n * 256, 256, 256)
+            EXS[e][rows, cols] = dot_t(BALL[e][rows, pl.ds(9 * COLS, 3 * COLS)], win[e, cols, :]).astype(BF16)
+
+        exchange(e, b, 1).start()
+
+    def token_end(e, b):
+        exchange(e, b, 1).wait()
+
+        @pl.loop(0, BLK[e] // CH)
+        def _(c):
+            rows = rows_at(b * BLK[e] + c * CH, CH, CH)
+            OB[e][rows, :] = (
+                N1[e][rows, :] + (EXS[e][rows, :].astype(F32) + EXR[e][1, rows, :].astype(F32))
+            ).astype(BF16)
+
+    def job_of(j):
+        return (j // 2) % 2, (j // 4) * 2 + j % 2
+
+    def product(e, half, blk, sel):
+        a = jnp.where(blk < 8, blk // 4, jnp.where(blk == 8, 2, 3)) * D
+        if half == 0:
+            rows = [AT[e][rows_at(a + i * 96 + sel * 48, 48), :] for i in range(8)]
+        else:
+            rows = [AT[e][rows_at(a + i * 192 + sel * 96, 96), :] for i in range(4)]
+        return dot(jnp.concatenate(rows, axis=0), BALL[e][:, rows_at(blk * COLS, COLS, 128)])
+
+    first_dev, other_dev = (at_x, at_y), (at_y, at_x)
+    first_at, other_at = (x, y), (y, x)
+
+    def p1(j, half):
+        return pltpu.make_async_remote_copy(
+            src_ref=p1s.at[j % DS, half],
+            dst_ref=p1r.at[j % D1, half],
+            send_sem=p1s_sem.at[j % DS, half],
+            recv_sem=p1r_sem.at[j % D1, half],
+            device_id=first_dev[half],
+            device_id_type=MESH_ID,
+        )
+
+    def along(j, half, d, right, relay):
+        buf, send, recv = (zr, zrs_sem, zrr_sem) if right else (zl, zls_sem, zlr_sem)
+        src = buf.at[j % DZ, half, d] if relay else p1r.at[j % D1, half, pl.ds(d * 96, 96)]
+        return pltpu.make_async_remote_copy(
+            src_ref=src,
+            dst_ref=buf.at[j % DZ, half, d],
+            send_sem=send.at[j % DZ, half, d],
+            recv_sem=recv.at[j % DZ, half, d],
+            device_id=at_dp(me + 4 if right else me - 4),
+            device_id_type=MESH_ID,
+        )
+
+    def p3(j, half):
+        return pltpu.make_async_remote_copy(
+            src_ref=p1r.at[j % D1, half, rows_at(z * 96 + (1 - other_at[half]) * 48, 48)],
+            dst_ref=p3r.at[j % D3, half],
+            send_sem=p3s_sem.at[j % D3, half],
+            recv_sem=p3r_sem.at[j % D3, half],
+            device_id=other_dev[half],
+            device_id_type=MESH_ID,
+        )
+
+    def add_into(dst, rows, other):
+        dst[rows, :] = (dst[rows, :].astype(F32) + other.astype(F32)).astype(BF16)
+
+    def step0(j):
+        e_of, pair = job_of(j)
+        for e in range(2):
+
+            @pl.when(e_of == e)
+            def _():
+                for half in range(2):
+                    p1s[j % DS, half] = product(e, half, pair * 2 + half, 1 - first_at[half]).astype(BF16)
+                    p1(j, half).start()
+
+    def step1(j):
+        e_of, pair = job_of(j)
+        for half in range(2):
+            p1(j, half).wait()
+        for e in range(2):
+
+            @pl.when(e_of == e)
+            def _():
+                for half in range(2):
+                    own = product(e, half, pair * 2 + half, first_at[half])
+                    p1r[j % D1, half] = (own + p1r[j % D1, half].astype(F32)).astype(BF16)
+
+        @pl.when(z == 0)
+        def _():
+            for half in range(2):
+                for d in (3, 2, 1):
+                    along(j, half, d, True, False).start()
+
+        @pl.when(z == 3)
+        def _():
+            for half in range(2):
+                for d in (0, 1, 2):
+                    along(j, half, d, False, False).start()
+
+    def relay(j, half, d, right):
+        buf = zr if right else zl
+        along(j, half, d, right, True).wait_recv()
+        add_into(buf.at[j % DZ, half, d], slice(None), p1r[j % D1, half, pl.ds(d * 96, 96), :])
+        along(j, half, d, right, True).start()
+
+    def step2(j):
+        @pl.when(z == 1)
+        def _():
+            for half in range(2):
+                for d in (3, 2):
+                    relay(j, half, d, True)
+
+        @pl.when(z == 2)
+        def _():
+            for half in range(2):
+                for d in (0, 1):
+                    relay(j, half, d, False)
+
+    def step3(j):
+        @pl.when(z == 2)
+        def _():
+            for half in range(2):
+                relay(j, half, 3, True)
+
+        @pl.when(z == 1)
+        def _():
+            for half in range(2):
+                relay(j, half, 0, False)
+
+    def step4(j):
+        for half in range(2):
+            mine = p1r.at[j % D1, half]
+            rows = rows_at(z * 96, 96)
+
+            @pl.when(z > 0)
+            def _():
+                along(j, half, z, True, True).wait_recv()
+                add_into(mine, rows, zr[j % DZ, half, z])
+
+            @pl.when(z < 3)
+            def _():
+                along(j, half, z, False, True).wait_recv()
+                add_into(mine, rows, zl[j % DZ, half, z])
+
+            p3(j, half).start()
+            for d in range(4):
+
+                @pl.when(d > z)
+                def _():
+                    along(j, half, d, True, True).wait_send()
+
+                @pl.when(d < z)
+                def _():
+                    along(j, half, d, False, True).wait_send()
+
+    def step5(j):
+        e_of, pair = job_of(j)
+        for half in range(2):
+            p3(j, half).wait()
+            rows = rows_at(z * 96 + other_at[half] * 48, 48)
+            total = p1r[j % D1, half, rows, :].astype(F32) + p3r[j % D3, half].astype(F32)
+            for e in range(2):
+                for p in range(6):
+
+                    @pl.when(jnp.logical_and(e_of == e, pair == p))
+                    def _():
+                        blk = p * 2 + half
+                        if blk < 4:
+                            g_fo[e, :, blk * COLS : (blk + 1) * COLS] = total
+                        elif blk < 8:
+                            g_fi[e, :, (blk - 4) * COLS : (blk - 3) * COLS] = total
+                        elif blk == 8:
+                            g_out[e] = total
+                        else:
+                            g_in[e, blk - 9] = total
+
+    small_to = (at_x, at_y, at_dp(me ^ 4), at_dp(me ^ 8))
+
+    def small(k):
+        return pltpu.make_async_remote_copy(
+            src_ref=smb.at[k],
+            dst_ref=smr.at[k],
+            send_sem=sms_sem.at[k],
+            recv_sem=smr_sem.at[k],
+            device_id=small_to[k],
+            device_id_type=MESH_ID,
+        )
+
+    def small_first():
+        smb[0] = jnp.zeros_like(smb[0])
+        for e in range(2):
+            for i in range(6):
+                smb[0, e * 9 + i : e * 9 + i + 1, :] = jnp.sum(acc_s[e * 6 + i], axis=0, keepdims=True)
+            smb[0, e * 9 + 6 : e * 9 + 7, :] = jnp.sum(acc_b[e], axis=0, keepdims=True)
+            for i in range(2):
+                smb[0, e * 9 + 7 + i : e * 9 + 8 + i, :] = jnp.sum(
+                    acc_f[e, :, i * D : (i + 1) * D], axis=0, keepdims=True
+                )
+        small(0).start()
+
+    def small_next(k):
+        small(k).wait()
+        if k < 3:
+            smb[k + 1] = smb[k] + smr[k]
+            small(k + 1).start()
+        else:
+            sm_out[...] = smb[k] + smr[k]
+
+    def both(body):
+        body(0, 0)
+        blocks(1, lambda b: body(1, b))
+
+    def all_token_end():
+        both(token_end)
+        pltpu.make_async_copy(obq, gq_out, out_sem.at[0]).start()
+        pltpu.make_async_copy(obp, gp_out, out_sem.at[1]).start()
+
+    def wait_out():
+        pltpu.make_async_copy(obq, oq_out, out_sem.at[0]).wait()
+        pltpu.make_async_copy(obp, op_out, out_sem.at[1]).wait()
+
+    work = {
+        0: [lambda: second_back(0, 0)],
+        1: [lambda: blocks(1, lambda b: second_back(1, b))],
+        2: [lambda: feed_back(0, 0)],
+        3: [lambda: blocks(1, lambda b: feed_back(1, b)), wait_out],
+        4: [lambda: first_back(0, 0)],
+        5: [lambda: blocks(1, lambda b: first_back(1, b))],
+        6: [lambda: attend_back(0, 0)],
+        7: [lambda: blocks(1, lambda b: attend_back(1, b))],
+        8: [lambda: both(token_back)],
+        9: [all_token_end],
+        10: [small_first],
+        11: [lambda: small_next(0)],
+        12: [lambda: small_next(1)],
+        13: [lambda: small_next(2)],
+        14: [lambda: small_next(3)],
+    }
+    steps = (step1, step2, step3, step4, step5)
+
+    @pl.loop(0, JOBS + 5)
+    def _(tick):
+        for at, things in work.items():
+
+            @pl.when(tick == at)
+            def _():
+                for thing in things:
+                    thing()
+
+        @pl.when(tick < JOBS)
+        def _():
+            step0(tick)
+
+        for late in (5, 4, 3, 2, 1):
+
+            @pl.when(jnp.logical_and(tick >= late, tick < JOBS + late))
+            def _():
+                steps[late - 1](tick - late)
+
+    pltpu.make_async_copy(obq, gq_out, out_sem.at[0]).wait()
+    pltpu.make_async_copy(obp, gp_out, out_sem.at[1]).wait()
+
+
+FF_HERE = 1536
+
+
+def fused(
+    question_tokens, passage_tokens, question_cotangent, passage_cotangent,
+    question_lengths, passage_lengths, dataset_ids, positives,
+    attn_in, attn_in_bias, attn_out, ffn_in, ffn_in_bias, ffn_out, out_biases, norm_gains, norm_shifts,
+):
+    any_spec = pl.BlockSpec(memory_space=pl.ANY)
+    vmem = pl.BlockSpec(memory_space=pltpu.VMEM)
+    smem = pl.BlockSpec(memory_space=pltpu.SMEM)
+
+    def both(shape, dtype):
+        return [pltpu.VMEM(shape(m), dtype) for m in TOKS]
+
+    shape = jax.ShapeDtypeStruct
+    dma = pltpu.SemaphoreType.DMA
+    outs = pl.pallas_call(
+        partial(fused_kernel, last=0),
+        name="fused",
+        in_specs=[any_spec] * 4 + [smem] * 4 + [any_spec, vmem, any_spec, any_spec, vmem, any_spec] + [vmem] * 3,
+        out_specs=[any_spec, any_spec, vmem, any_spec, any_spec] + [vmem] * 5,
+        out_shape=[
+            shape((128, D), BF16),
+            shape((512, D), BF16),
+            shape((8, 128), F32),
+            shape((128, D), BF16),
+            shape((512, D), BF16),
+            shape((2, 3, ROWS_OUT, COLS), F32),
+            shape((2, ROWS_OUT, COLS), F32),
+            shape((2, ROWS_OUT, FF_HERE), F32),
+            shape((2, ROWS_OUT, FF_HERE), F32),
+            shape((SMALL, D), F32),
+        ],
+        scratch_shapes=[
+            pltpu.VMEM((2, D, 3 * COLS), BF16),
+            pltpu.VMEM((2, COLS, D), BF16),
+            pltpu.VMEM((2, D, FF_HERE), BF16),
+            pltpu.VMEM((2, FF_HERE, D), BF16),
+            *both(lambda m: (m, D), BF16),
+            *both(lambda m: (m, D), BF16),
+            *both(lambda m: (m, 3 * COLS), BF16),
+            pltpu.VMEM((1, 6, 128, 128), BF16),
+            pltpu.VMEM((2, 6, 256, 256), BF16),
+            *both(lambda m: (m, D), BF16),
+            *both(lambda m: (m, D), F32),
+            *both(lambda m: (m, D), F32),
+            *both(lambda m: (m, 1), F32),
+            *both(lambda m: (m, 1), F32),
+            *both(lambda m: (m, FF_HERE), BF16),
+            *both(lambda m: (m, D), BF16),
+            *both(lambda m: (m, D), BF16),
+            *both(lambda m: (m, COLS), BF16),
+            *both(lambda m: (m, 12 * COLS), BF16),
+            *both(lambda m: (4 * D, m), BF16),
+            *both(lambda m: (m, D), BF16),
+            *both(lambda m: (2, m, D), BF16),
+            pltpu.VMEM((16, D), F32),
+            pltpu.VMEM((8, COLS), F32),
+            pltpu.VMEM((8, FF_HERE), F32),
+            pltpu.VMEM((64, 32), F32),
+            pltpu.VMEM((16, 16, 256), BF16),
+            pltpu.VMEM((2, 256, 128), F32),
+            pltpu.VMEM((64, D), F32),
+            pltpu.VMEM((12, 8, D), F32),
+            pltpu.VMEM((2, 8, 2 * COLS), F32),
+            pltpu.VMEM((2, 8, FF_HERE), F32),
+            pltpu.VMEM((4, SMALL, D), F32),
+            pltpu.VMEM((4, SMALL, D), F32),
+            pltpu.VMEM((DS, 2, COLS, COLS), BF16),
+            pltpu.VMEM((D1, 2, COLS, COLS), BF16),
+            pltpu.VMEM((DZ, 2, ZN, 96, COLS), BF16),
+            pltpu.VMEM((DZ, 2, ZN, 96, COLS), BF16),
+            pltpu.VMEM((D3, 2, ROWS_OUT, COLS), BF16),
+            dma((16,)),
+            dma((2,)),
+            dma((3,)),
+            dma((2, 3)),
+            dma((16,)),
+            dma((16,)),
+            dma((4,)),
+            dma((4,)),
+            dma((DS, 2)),
+            dma((D1, 2)),
+            dma((DZ, 2, ZN)),
+            dma((DZ, 2, ZN)),
+            dma((DZ, 2, ZN)),
+            dma((DZ, 2, ZN)),
+            dma((D3, 2)),
+            dma((D3, 2)),
+        ],
+        compiler_params=pltpu.CompilerParams(
+            collective_id=0, has_side_effects=True, vmem_limit_bytes=VMEM_BYTES
+        ),
+    )(
+        question_tokens.reshape(128, D),
+        passage_tokens.reshape(512, D),
+        question_cotangent.reshape(128, D),
+        passage_cotangent.reshape(512, D),
+        question_lengths, passage_lengths, dataset_ids, positives,
+        attn_in.transpose(0, 2, 1, 3), attn_in_bias, attn_out, ffn_in, ffn_in_bias, ffn_out,
+        out_biases, norm_gains, norm_shifts,
+    )
+    oq, op, loss, gq, gp, g_in, g_out, g_fi, g_fo, sums = outs
+    me = lax.axis_index("dp")
+    sums = sums[:18].reshape(2, 9, D)
+    wide = lax.dynamic_slice_in_dim(sums[:, 0:6], me * ROWS_OUT, ROWS_OUT, axis=2)
+    in_bias = lax.dynamic_slice_in_dim(sums[:, 6].reshape(2, 2, COLS), me * 24, 24, axis=2)
+    fi_bias = lax.dynamic_slice_in_dim(sums[:, 7:9].reshape(2, FF_HERE), me * 96, 96, axis=1)
+    return (
+        oq.reshape(2, 64, D),
+        op.reshape(2, 256, D),
+        loss[0, 0],
+        gq.reshape(2, 64, D),
+        gp.reshape(2, 256, D),
+        g_in.transpose(0, 2, 1, 3),
+        in_bias,
+        g_out.transpose(0, 2, 1),
+        g_fi,
+        fi_bias,
+        g_fo.transpose(0, 2, 1),
+        wide[:, 4:6],
+        wide[:, 0:2],
+        wide[:, 2:4],
+    )
+
+
+VMEM_BYTES = 62 * 1024 * 1024
+
+
 def solution(mesh):
     in_specs = (
         P("dp", None, None),
@@ -395,6 +1247,7 @@
         P(None, None, "dp"),
         P(None, None, "dp"),
     )
+    step = fused if mesh.shape["dp"] == 4 * ZN and mesh.shape["tensor"] == 2 else per_device
     return jax.shard_map(
-        per_device, mesh=mesh, in_specs=in_specs, out_specs=out_specs, check_vma=False
-    )
+        step, mesh=mesh, in_specs=in_specs, out_specs=out_specs, check_vma=False
+    )

time: 2240 us -> 194 us (0.09)
  waiting for transfers between devices: 1860 us -> 0 us
  Pallas kernels: 0 us -> 177 us
  blocking collectives: 131 us -> 0 us
  matrix products: 86.1 us -> 0 us
  other arithmetic: 69.3 us -> 0 us
  local copies, waits for them, and re-layouts: 67.4 us -> 15.7 us
    unnamed x26 -> x0, waiting for transfers between devices: 983 us -> none
    reduce_scatter x6 -> x0, waiting for transfers between devices: 818 us -> none  [the longest x1 143 us: per_device(): lax.psum_scatter(passage_weights[3], 'dp', scatter_dimension=0, tiled=True)]
    pallas_call x0 -> x1, Pallas kernels: none -> 177 us  [fused(): pl.pallas_call(partial(fused_kernel, last=0), name='fused', in_specs=[any...]
    dot_general x39 -> x0, matrix products: 86.1 us -> none  [the longest x2 9.45 us: encoder_backward(): jnp.einsum('bld,fd->blf', d_down, ffn_out, preferred_element_type=jnp.flo...]
    psum x1 -> x0, blocking collectives: 77.1 us -> none  [per_device(): total = lax.psum(jnp.sum(cross), 'dp')]
    psum x4 -> x0, waiting for transfers between devices: 62.8 us -> none  [the longest x1 19.3 us: encoder_backward(): lax.psum(token_part.astype(jnp.bfloat16), 'tensor').astype(jnp.float32)]
    all_gather x1 -> x0, blocking collectives: 54.1 us -> none  [per_device(): all_passages = lax.all_gather(passage_heads, 'dp', axis=0, tiled=True)]
    reduce_sum x19 -> x0, other arithmetic: 28.8 us -> none  [the longest x4 9.4 us: norm_backward(): jnp.sum(incoming * normed, axis=(0, 1))]
  transfers between devices with their start and end apart: 18 -> 0, of which waited for: 17 -> 0; matrix products, arithmetic and copies ran while one was open for 4% -> 0% of each run, Pallas kernels for 0% -> 0%
where the time goes in v1:
time: 194 us; the launch traced here: 193 us
  Pallas kernels  177 us (91%)
  local copies, waits for them, and re-layouts  15.7 us (8%)
    pallas_call x1, Pallas kernels, fused(): pl.pallas_call(partial(fused_kernel, last=0), name='fused', in_specs=[any...  177 us
    unnamed x16, local copies, waits for them, and re-layouts  11.5 us

profile of v1, /device:TPU:0, one launch (start us, length us, event | category | flops | bytes accessed | tf_op | source)
XLA Modules:
  0.0 193.4 jit_solution(11752616939105746490)
XLA Ops:
  0.7 177.0 %fused.1 = (bf16[128,768]{1,0:T(8,128)(2,1)}, bf16[512,768]{1,0:T(8,128)(2,1)}, f32[8,128]{1,0:T(8,128)}, bf16[128,768]{1,0:T(8,128)(2,1)}, bf16[512,768]{1,0:T(...) custom-call(bf16[128,768]{1,0:T(8,128)(2,1)} %bitcast.24, ...), custom_call_target="tpu_custom_call" | custom-call | tf_op jit(solution)/shard_map/fused/pallas_call | solution.py:1101
  177.7 0.0 copy-start.2
  177.7 0.0 copy-start.1
  177.7 0.0 copy-start
  177.7 1.0 reshape.66
  178.7 0.7 constant_dynamic-slice_fusion.2
  179.4 0.6 constant_dynamic-slice_fusion.3
  180.1 0.7 constant_dynamic-slice_fusion.4
  180.8 1.2 slice.24
  182.0 1.6 copy.40
  183.6 2.1 %copy.41 = bf16[2,256,768]{2,1,0:T(8,128)(2,1)} copy(bf16[2,256,768]{2,1,0:T(8,128)(2,1)} %bitcast.21) | data formatting | bytes 1572864
  185.7 1.6 copy.42
  187.3 2.1 %copy.43 = bf16[2,256,768]{2,1,0:T(8,128)(2,1)} copy(bf16[2,256,768]{2,1,0:T(8,128)(2,1)} %bitcast.20) | data formatting | bytes 1572864
  189.3 1.8 copy.44
  191.1 0.0 copy-done.2
  191.1 0.7 copy.45
  191.8 0.0 copy-done.1
  191.8 0.8 copy.46
  192.6 0.0 copy-done
  192.6 0.8 copy.47
  (5 shorter events, 0.1 us)
Async XLA Ops:
  177.7 13.4 %copy-start.2 = (f32[2,48,384]{2,1,0:T(8,128)S(1)}, f32[2,48,384]{2,1,0:T(8,128)}, u32[]{:S(2)}) copy-start(f32[2,48,384]{2,1,0:T(8,128)} %get-tuple-element.31) | copy-start | bytes 442372
  177.7 14.1 %copy-start.1 = (f32[2,48,1536]{2,1,0:T(8,128)S(1)}, f32[2,48,1536]{2,1,0:T(8,128)}, u32[]{:S(2)}) copy-start(f32[2,48,1536]{2,1,0:T(8,128)} %get-tuple-element.59) | copy-start | bytes 1769476
  177.7 14.9 %copy-start = (f32[2,48,1536]{2,1,0:T(8,128)S(1)}, f32[2,48,1536]{2,1,0:T(8,128)}, u32[]{:S(2)}) copy-start(f32[2,48,1536]{2,1,0:T(8,128)} %get-tuple-element.33) | copy-start | bytes 1769476

commit v2 on v1

--- a/solution.py
+++ b/solution.py
@@ -418,8 +418,8 @@
     win, wo, wf, wd, xq, xp, cq, cp, qkvq, qkvp, prq, prp, hq, hp, n1q, n1p, n2q, n2p,
     i1q, i1p, i2q, i2p, sq, sp, obq, obp, ddq, ddp, dcq, dcp, ballq, ballp, atq, atp,
     exsq, exsp, exrq, exrp, par, pin, pfi, masks, hg, hf, dh, acc_s, acc_b, acc_f, smb, smr,
-    p1s, p1r, zr, zl, p3r,
-    in_sem, out_sem, exs_sem, exr_sem, hgs_sem, hgr_sem, sms_sem, smr_sem,
+    p1s, p1r, zr, zl, p3r, fin,
+    fin_sem, in_sem, out_sem, exs_sem, exr_sem, hgs_sem, hgr_sem, sms_sem, smr_sem,
     p1s_sem, p1r_sem, zrs_sem, zrr_sem, zls_sem, zlr_sem, p3s_sem, p3r_sem,
     *, last,
 ):
@@ -973,12 +973,21 @@
                 def _():
                     along(j, half, d, False, True).wait_send()
 
+    def result(slot, half, to):
+        return pltpu.make_async_copy(fin.at[slot, half], to, fin_sem.at[slot, half])
+
     def step5(j):
         e_of, pair = job_of(j)
         for half in range(2):
             p3(j, half).wait()
             rows = rows_at(z * 96 + other_at[half] * 48, 48)
             total = p1r[j % D1, half, rows, :].astype(F32) + p3r[j % D3, half].astype(F32)
+
+            @pl.when(j >= 2)
+            def _():
+                result(j % 2, half, g_out.at[0]).wait()
+
+            fin[j % 2, half] = total
             for e in range(2):
                 for p in range(6):
 
@@ -986,13 +995,14 @@
                     def _():
                         blk = p * 2 + half
                         if blk < 4:
-                            g_fo[e, :, blk * COLS : (blk + 1) * COLS] = total
+                            to = g_fo.at[e, :, pl.ds(blk * COLS, COLS)]
                         elif blk < 8:
-                            g_fi[e, :, (blk - 4) * COLS : (blk - 3) * COLS] = total
+                            to = g_fi.at[e, :, pl.ds((blk - 4) * COLS, COLS)]
                         elif blk == 8:
-                            g_out[e] = total
+                            to = g_out.at[e]
                         else:
-                            g_in[e, blk - 9] = total
+                            to = g_in.at[e, blk - 9]
+                        result(j % 2, half, to).start()
 
     small_to = (at_x, at_y, at_dp(me ^ 4), at_dp(me ^ 8))
 
@@ -1024,7 +1034,18 @@
             smb[k + 1] = smb[k] + smr[k]
             small(k + 1).start()
         else:
-            sm_out[...] = smb[k] + smr[k]
+            total = smb[k] + smr[k]
+            sm_out[...] = jnp.zeros_like(sm_out)
+            wide = pltpu.roll(total, lax.rem(D - me * ROWS_OUT, D), 1)
+            sm_out[:, 0:ROWS_OUT] = wide[:, 0:ROWS_OUT]
+            heads_own = pltpu.roll(total, lax.rem(D - me * 24, D), 1)
+            feed_own = pltpu.roll(total, lax.rem(D - (me % 8) * 96, D), 1)
+            for e in range(2):
+                at = e * 9 + 6
+                for i in range(2):
+                    sm_out[at + i : at + i + 1, 0:24] = heads_own[at : at + 1, i * COLS : i * COLS + 24]
+                low, high = feed_own[at + 1 : at + 2, 0:96], feed_own[at + 2 : at + 3, 0:96]
+                sm_out[at + 2 : at + 3, 0:96] = jnp.where(me < 8, low, high)
 
     def both(body):
         body(0, 0)
@@ -1079,6 +1100,33 @@
 
     pltpu.make_async_copy(obq, gq_out, out_sem.at[0]).wait()
     pltpu.make_async_copy(obp, gp_out, out_sem.at[1]).wait()
+    for slot in range(2):
+        for half in range(2):
+            result(slot, half, g_out.at[0]).wait()
+
+
+def finish_kernel(*refs):
+    oq, op, gq, gp, g_in, g_out, g_fi, g_fo, loss, sums = refs[:10]
+    large, (loss_to, in_bias, fi_bias, bo, gain, shift) = refs[10:18], refs[18:24]
+    held, in_sems, out_sems = refs[24:32], refs[32], refs[33]
+    sources = (oq, op, gq, gp, g_in, g_out, g_fi, g_fo)
+    loads = [pltpu.make_async_copy(sources[i], held[i], in_sems.at[i]) for i in range(8)]
+    stores = [pltpu.make_async_copy(held[i], large[i], out_sems.at[i]) for i in range(8)]
+    for load in loads:
+        load.start()
+    loss_to[...] = loss[0:1, 0:1]
+    for e in range(2):
+        at = e * 9
+        gain[e] = sums[at : at + 2, 0:ROWS_OUT]
+        shift[e] = sums[at + 2 : at + 4, 0:ROWS_OUT]
+        bo[e] = sums[at + 4 : at + 6, 0:ROWS_OUT]
+        in_bias[e] = sums[at + 6 : at + 8, 0:24]
+        fi_bias[e : e + 1] = sums[at + 8 : at + 9, 0:96]
+    for load, store in zip(loads, stores):
+        load.wait()
+        store.start()
+    for store in stores:
+        store.wait()
 
 
 FF_HERE = 1536
@@ -1102,7 +1150,7 @@
         partial(fused_kernel, last=0),
         name="fused",
         in_specs=[any_spec] * 4 + [smem] * 4 + [any_spec, vmem, any_spec, any_spec, vmem, any_spec] + [vmem] * 3,
-        out_specs=[any_spec, any_spec, vmem, any_spec, any_spec] + [vmem] * 5,
+        out_specs=[any_spec, any_spec, vmem] + [any_spec] * 6 + [vmem],
         out_shape=[
             shape((128, D), BF16),
             shape((512, D), BF16),
@@ -1113,7 +1161,7 @@
             shape((2, ROWS_OUT, COLS), F32),
             shape((2, ROWS_OUT, FF_HERE), F32),
             shape((2, ROWS_OUT, FF_HERE), F32),
-            shape((SMALL, D), F32),
+            shape((SMALL, 128), F32),
         ],
         scratch_shapes=[
             pltpu.VMEM((2, D, 3 * COLS), BF16),
@@ -1155,6 +1203,8 @@
             pltpu.VMEM((DZ, 2, ZN, 96, COLS), BF16),
             pltpu.VMEM((DZ, 2, ZN, 96, COLS), BF16),
             pltpu.VMEM((D3, 2, ROWS_OUT, COLS), BF16),
+            pltpu.VMEM((2, 2, ROWS_OUT, COLS), F32),
+            dma((2, 2)),
             dma((16,)),
             dma((2,)),
             dma((3,)),
@@ -1185,15 +1235,21 @@
         out_biases, norm_gains, norm_shifts,
     )
     oq, op, loss, gq, gp, g_in, g_out, g_fi, g_fo, sums = outs
-    me = lax.axis_index("dp")
-    sums = sums[:18].reshape(2, 9, D)
-    wide = lax.dynamic_slice_in_dim(sums[:, 0:6], me * ROWS_OUT, ROWS_OUT, axis=2)
-    in_bias = lax.dynamic_slice_in_dim(sums[:, 6].reshape(2, 2, COLS), me * 24, 24, axis=2)
-    fi_bias = lax.dynamic_slice_in_dim(sums[:, 7:9].reshape(2, FF_HERE), me * 96, 96, axis=1)
+    large = (oq, op, gq, gp, g_in, g_out, g_fi, g_fo)
+    small = [(1, 1), (2, 2, 24), (2, 96), (2, 2, ROWS_OUT), (2, 2, ROWS_OUT), (2, 2, ROWS_OUT)]
+    oq, op, gq, gp, g_in, g_out, g_fi, g_fo, loss, in_bias, fi_bias, bo, gain, shift = pl.pallas_call(
+        finish_kernel,
+        name="finish",
+        in_specs=[any_spec] * 8 + [vmem] * 2,
+        out_specs=[any_spec] * 8 + [vmem] * 6,
+        out_shape=[shape(a.shape, a.dtype) for a in large] + [shape(dims, F32) for dims in small],
+        scratch_shapes=[*[pltpu.VMEM(a.shape, a.dtype) for a in large], dma((8,)), dma((8,))],
+        compiler_params=pltpu.CompilerParams(vmem_limit_bytes=VMEM_BYTES),
+    )(*large, loss, sums)
     return (
         oq.reshape(2, 64, D),
         op.reshape(2, 256, D),
-        loss[0, 0],
+        loss.reshape(()),
         gq.reshape(2, 64, D),
         gp.reshape(2, 256, D),
         g_in.transpose(0, 2, 1, 3),
@@ -1202,9 +1258,9 @@
         g_fi,
         fi_bias,
         g_fo.transpose(0, 2, 1),
-        wide[:, 4:6],
-        wide[:, 0:2],
-        wide[:, 2:4],
+        bo,
+        gain,
+        shift,
     )
 
 

time: 194 us -> 183 us (0.943)
  local copies, waits for them, and re-layouts: 15.7 us -> 0 us
  Pallas kernels: 177 us -> 182 us
    unnamed x16 -> x0, local copies, waits for them, and re-layouts: 11.5 us -> none
    pallas_call x0 -> x1, Pallas kernels: none -> 4.49 us  [fused(): pl.pallas_call(finish_kernel, name='finish', in_specs=[any_spec] * 8 + [v...]
where the time goes in v2:
time: 183 us; the launch traced here: 182 us
  Pallas kernels  182 us (99%)
    pallas_call x1, Pallas kernels, fused(): pl.pallas_call(partial(fused_kernel, last=0), name='fused', in_specs=[any...  177 us
    pallas_call x1, Pallas kernels, fused(): pl.pallas_call(finish_kernel, name='finish', in_specs=[any_spec] * 8 + [v...  4.49 us

profile of v2, /device:TPU:0, one launch (start us, length us, event | category | flops | bytes accessed | tf_op | source)
XLA Modules:
  0.0 182.3 jit_solution(14012422502532600969)
XLA Ops:
  0.7 177.1 %fused.1 = (bf16[128,768]{1,0:T(8,128)(2,1)}, bf16[512,768]{1,0:T(8,128)(2,1)}, f32[8,128]{1,0:T(8,128)}, bf16[128,768]{1,0:T(8,128)(2,1)}, bf16[512,768]{1,0:T(...) custom-call(bf16[128,768]{1,0:T(8,128)(2,1)} %bitcast.16, ...), custom_call_target="tpu_custom_call" | custom-call | tf_op jit(solution)/shard_map/fused/pallas_call | solution.py:1149
  177.8 4.5 %finish.1 = (bf16[128,768]{1,0:T(8,128)(2,1)}, bf16[512,768]{1,0:T(8,128)(2,1)}, bf16[128,768]{1,0:T(8,128)(2,1)}, bf16[512,768]{1,0:T(8,128)(2,1)}, f32[2,3,48,...) custom-call(bf16[128,768]{1,0:T(8,128)(2,1)} %get-tuple-element.38.r, ...), custom_call_target="tpu_custom_call" | custom-call | tf_op jit(solution)/shard_map/finish/pallas_call | solution.py:1240

commit v3 on v2

--- a/solution.py
+++ b/solution.py
@@ -368,7 +368,8 @@
 ROWS_OUT = 48
 JOBS = 12
 COLS = 384
-D1, DZ, D3, DS = 8, 4, 2, 2
+D1, D2, DZ, DS = 8, 6, 5, 2
+LINE_FIRST = (6, 8, 9, 11)
 TOKS = (128, 512)
 BLK = (128, 256)
 SMALL = 24
@@ -418,9 +419,10 @@
     win, wo, wf, wd, xq, xp, cq, cp, qkvq, qkvp, prq, prp, hq, hp, n1q, n1p, n2q, n2p,
     i1q, i1p, i2q, i2p, sq, sp, obq, obp, ddq, ddp, dcq, dcp, ballq, ballp, atq, atp,
     exsq, exsp, exrq, exrp, par, pin, pfi, masks, hg, hf, dh, acc_s, acc_b, acc_f, smb, smr,
-    p1s, p1r, zr, zl, p3r, fin,
+    p1s, p1r, p2r, zr, zl, fin, fra, frb, xms, xmr, hm, am,
     fin_sem, in_sem, out_sem, exs_sem, exr_sem, hgs_sem, hgr_sem, sms_sem, smr_sem,
-    p1s_sem, p1r_sem, zrs_sem, zrr_sem, zls_sem, zlr_sem, p3s_sem, p3r_sem,
+    p1s_sem, p1r_sem, p2s_sem, p2r_sem, zrs_sem, zrr_sem, zls_sem, zlr_sem,
+    fas_sem, far_sem, fbs_sem, fbr_sem, xms_sem, xmr_sem,
     *, last,
 ):
     me = lax.axis_index("dp")
@@ -521,11 +523,10 @@
         else:
             pl.loop(0, 2)(body)
 
-    def attend(e, b):
-        size = BLK[e]
+    def project(e, b, which):
         rows = block_rows(e, b)
         xb = X[e][rows, :]
-        for j in range(3):
+        for j in which:
             cols = pl.ds(j * COLS, COLS)
             got = dot(xb, win[e, :, cols])
             if j == 0:
@@ -534,6 +535,9 @@
                 got = got + pin[e * 2 + 1 : e * 2 + 2, :]
             QKV[e][rows, cols] = got.astype(BF16)
 
+    def attend(e, b):
+        size = BLK[e]
+        rows = block_rows(e, b)
         col = lax.broadcasted_iota(jnp.int32, (size, size), 1)
         if e == 0:
             row = lax.broadcasted_iota(jnp.int32, (size, size), 0)
@@ -624,31 +628,125 @@
                 n * par[e * 8 + 3 : e * 8 + 4, :] + par[e * 8 + 5 : e * 8 + 6, :]
             ).astype(BF16)
 
+    def mini_exchange(k):
+        return pltpu.make_async_remote_copy(
+            src_ref=xms.at[k],
+            dst_ref=xmr.at[k],
+            send_sem=xms_sem.at[k],
+            recv_sem=xmr_sem.at[k],
+            device_id=partner,
+            device_id_type=MESH_ID,
+        )
+
+    def first_rows(ref):
+        rows = [ref[b * 256 : b * 256 + 16, :].astype(F32)[0:1] for b in range(2)]
+        return jnp.concatenate([*rows, jnp.zeros((14, rows[0].shape[1]), F32)], axis=0)
+
+    def mini_attend():
+        xm = first_rows(xp).astype(BF16)
+        q = (dot(xm, win[1, :, pl.ds(0, COLS)]) + pin[2:3, :]).astype(BF16).astype(F32) * HD**-0.5
+        of_head = lax.broadcasted_iota(jnp.int32, (16, COLS), 1) // HD == lax.broadcasted_iota(
+            jnp.int32, (16, COLS), 0
+        )
+        col = lax.broadcasted_iota(jnp.int32, (16, 256), 1)
+        rows = []
+        for b in range(2):
+            keys = qkvp[b * 256 : (b + 1) * 256, COLS : 2 * COLS]
+            vals = qkvp[b * 256 : (b + 1) * 256, 2 * COLS : 3 * COLS]
+            s = dot_t(jnp.where(of_head, q[b : b + 1], 0.0).astype(BF16), keys)
+            s = jnp.where(col < plen[b], s, NEGATIVE)
+            p = jnp.exp(s - jnp.max(s, axis=-1, keepdims=True))
+            p = (p * (1.0 / jnp.sum(p, axis=-1, keepdims=True))).astype(BF16)
+            rows.append(jnp.sum(jnp.where(of_head, dot(p, vals), 0.0), axis=0, keepdims=True))
+        ctx = jnp.concatenate([*rows, jnp.zeros((14, COLS), F32)], axis=0)
+        xms[0] = dot(ctx.astype(BF16), wo[1]).astype(BF16)
+        mini_exchange(0).start()
+
+    def mini_norm(k, v):
+        mini_exchange(k).wait()
+        v = v + (xms[k].astype(F32) + xmr[k].astype(F32)) + par[8 + k : 9 + k, :]
+        v = v - row_mean(v)
+        n = v * lax.rsqrt(row_mean(v * v) + EPSILON)
+        return (n * par[10 + k : 11 + k, :] + par[12 + k : 13 + k, :]).astype(BF16)
+
+    def mini_feed():
+        hm[...] = mini_norm(0, first_rows(xp))
+
+        @pl.loop(0, 6)
+        def _(n):
+            cols = rows_at(n * 256, 256, 256)
+            u = dot(hm[...], wf[1, :, cols]) + pfi[1:2, cols]
+            am[:, cols] = gelu_and_slope(u)[0].astype(BF16)
+
+        @pl.loop(0, 3)
+        def _(n):
+            cols = rows_at(n * 256, 256, 256)
+            xms[1, :, cols] = dot(am[...], wd[1, :, cols]).astype(BF16)
+
+        mini_exchange(1).start()
+
+    def transpose_into(e, k, src, b):
+        rows = block_rows(e, b)
+
+        @pl.loop(0, 2)
+        def _(c):
+            tile = src[rows, rows_at(c * COLS, COLS, 128)].T
+            AT[e][k, pl.ds(c * 2, 2), :, :, :, rows] = tile.reshape(2, 2, 2, ROWS_OUT, BLK[e])
+
+    def left_factor(axis, k):
+        return pltpu.make_async_remote_copy(
+            src_ref=atq.at[k, :, :, 1 - x] if axis == 0 else atq.at[k, :, 1 - y],
+            dst_ref=fra.at[axis, k],
+            send_sem=fas_sem.at[axis, k],
+            recv_sem=far_sem.at[axis, k],
+            device_id=first_dev[axis],
+            device_id_type=MESH_ID,
+        )
+
+    def right_factor(axis, pair):
+        return pltpu.make_async_remote_copy(
+            src_ref=ballq.at[:, pl.ds((pair * 2 + axis) * COLS, COLS)],
+            dst_ref=frb.at[axis, pair],
+            send_sem=fbs_sem.at[axis, pair],
+            recv_sem=fbr_sem.at[axis, pair],
+            device_id=first_dev[axis],
+            device_id_type=MESH_ID,
+        )
+
+    first_dev, other_dev = (at_x, at_y), (at_y, at_x)
+    first_at, other_at = (x, y), (y, x)
+
     need(0, 1, 2, 3, 8)
     pl.semaphore_wait(barrier, 16)
+    project(0, 0, (0, 1, 2))
     attend(0, 0)
+    right_factor(0, 4).start()
     need(4, 5, 6, 7, 9)
-    blocks(1, lambda b: attend(1, b))
+    blocks(1, lambda b: project(1, b, (1, 2)))
+    mini_attend()
+    transpose_into(0, 3, xq, 0)
+    left_factor(0, 3).start()
+    left_factor(1, 3).start()
     first_norm(0, 0)
     need(10, 12)
     feed(0, 0)
+    for axis in range(2):
+        for pair in range(2):
+            right_factor(axis, pair).start()
     need(11, 13)
-
-    def passage_mid(b):
-        first_norm(1, b)
-        feed(1, b)
-
-    blocks(1, passage_mid)
+    mini_feed()
+    transpose_into(0, 1, hq, 0)
+    left_factor(0, 1).start()
+    left_factor(1, 1).start()
     second_norm(0, 0)
-    blocks(1, lambda b: second_norm(1, b))
     out_q = pltpu.make_async_copy(obq, oq_out, out_sem.at[0])
     out_p = pltpu.make_async_copy(obp, op_out, out_sem.at[1])
     out_q.start()
-    out_p.start()
+    mini_out = mini_norm(1, hm[...].astype(F32)).astype(F32)
 
     pieces = []
-    for ref, at in ((obq, 0), (obq, 64), (obp, 0), (obp, 256)):
-        head = ref[at : at + 16, :].astype(F32)[0:1]
+    rows = [obq[at : at + 16, :].astype(F32)[0:1] for at in (0, 64)]
+    for head in (*rows, mini_out[0:1], mini_out[1:2]):
         pieces += [head[:, k * 256 : (k + 1) * 256] for k in range(3)]
     pieces.append(jnp.zeros((4, 256), F32))
     hg[me] = jnp.concatenate(pieces, axis=0).astype(BF16)
@@ -666,6 +764,8 @@
     for k in range(1, 16):
         heads(k).start()
     need(14, 15)
+    blocks(1, lambda b: project(1, b, (0,)))
+    attend(1, 0)
     for k in range(1, 16):
         copy = pltpu.make_async_remote_copy(
             src_ref=hg.at[me],
@@ -711,14 +811,6 @@
         scaled = incoming * scale
         return inv * (scaled - row_mean(scaled) - n * row_mean(scaled * n))
 
-    def transpose_into(e, k, src, b, width=D):
-        rows = block_rows(e, b)
-
-        @pl.loop(0, width // 256)
-        def _(c):
-            tile = src[rows, rows_at(c * 256, 256, 256)]
-            AT[e][rows_at(k * D + c * 256, 256, 256), rows] = tile.T
-
     def second_back(e, b):
         row0 = lax.broadcasted_iota(jnp.int32, (CH, 1), 0)
         seqs = 2 if e == 0 else 1
@@ -760,7 +852,8 @@
             EXS[e][rows, cols] = dot_t(BALL[e][rows, pl.ds(4 * COLS, FF_HERE)], wf[e, cols, :]).astype(BF16)
 
         exchange(e, b, 0).start()
-        transpose_into(e, 1, HID[e], b)
+        if e == 1:
+            transpose_into(e, 1, HID[e], b)
 
     def first_back(e, b):
         exchange(e, b, 0).wait()
@@ -812,7 +905,8 @@
             acc_b[e, :, cols] += fold8(dq.astype(F32))
             acc_b[e, :, rows_at(COLS + pair * 128, 128, 128)] += fold8(dv.astype(F32))
 
-        transpose_into(e, 3, X[e], b)
+        if e == 1:
+            transpose_into(e, 3, X[e], b)
 
     def token_back(e, b):
         rows = block_rows(e, b)
@@ -835,18 +929,21 @@
             ).astype(BF16)
 
     def job_of(j):
-        return (j // 2) % 2, (j // 4) * 2 + j % 2
-
-    def product(e, half, blk, sel):
-        a = jnp.where(blk < 8, blk // 4, jnp.where(blk == 8, 2, 3)) * D
-        if half == 0:
-            rows = [AT[e][rows_at(a + i * 96 + sel * 48, 48), :] for i in range(8)]
-        else:
-            rows = [AT[e][rows_at(a + i * 192 + sel * 96, 96), :] for i in range(4)]
-        return dot(jnp.concatenate(rows, axis=0), BALL[e][:, rows_at(blk * COLS, COLS, 128)])
-
-    first_dev, other_dev = (at_x, at_y), (at_y, at_x)
-    first_at, other_at = (x, y), (y, x)
+        return j // 6, j % 6
+
+    def product(half, blk, sel):
+        k = jnp.where(blk < 8, blk // 4, jnp.where(blk == 8, 2, 3))
+        rows = atp[k, :, :, sel] if half == 0 else atp[k, :, sel]
+        out = dot(rows.reshape(COLS, TOKS[1]), ballp[:, rows_at(blk * COLS, COLS, 128)])
+        return out.reshape(ZN, 2, ROWS_OUT, COLS)
+
+    def pair_product(half, pair):
+        blk = pair * 2 + half
+        k = blk // 4 if blk < 8 else 2 if blk == 8 else 3
+        rows = atq[k, :, :, x] if half == 0 else atq[k, :, y]
+        rows = jnp.concatenate([rows.reshape(COLS, TOKS[0]), fra[half, k].reshape(COLS, TOKS[0])], axis=1)
+        cols = jnp.concatenate([ballq[:, blk * COLS : (blk + 1) * COLS], frb[half, pair]], axis=0)
+        return dot(rows, cols).reshape(ZN, 2, ROWS_OUT, COLS)
 
     def p1(j, half):
         return pltpu.make_async_remote_copy(
@@ -858,135 +955,169 @@
             device_id_type=MESH_ID,
         )
 
-    def along(j, half, d, right, relay):
+    def other(j, half, line_first):
+        mine, to = p1r.at[j % D1, half], p2r.at[j % D2, half]
+        return pltpu.make_async_remote_copy(
+            src_ref=mine.at[z, 1 - other_at[half]] if line_first else mine.at[:, 1 - other_at[half]],
+            dst_ref=to.at[0] if line_first else to,
+            send_sem=p2s_sem.at[j % D2, half],
+            recv_sem=p2r_sem.at[j % D2, half],
+            device_id=other_dev[half],
+            device_id_type=MESH_ID,
+        )
+
+    def block(ref, j, half, d, line_first):
+        return ref.at[j % DZ, half, d] if line_first else ref.at[j % DZ, half, d, 0]
+
+    def own_block(j, half, d, line_first):
+        return p1r.at[j % D1, half, d] if line_first else p2r.at[j % D2, half, d]
+
+    def along(j, half, d, right, relayed, line_first):
         buf, send, recv = (zr, zrs_sem, zrr_sem) if right else (zl, zls_sem, zlr_sem)
-        src = buf.at[j % DZ, half, d] if relay else p1r.at[j % D1, half, pl.ds(d * 96, 96)]
+        there = block(buf, j, half, d, line_first)
         return pltpu.make_async_remote_copy(
-            src_ref=src,
-            dst_ref=buf.at[j % DZ, half, d],
+            src_ref=there if relayed else own_block(j, half, d, line_first),
+            dst_ref=there,
             send_sem=send.at[j % DZ, half, d],
             recv_sem=recv.at[j % DZ, half, d],
             device_id=at_dp(me + 4 if right else me - 4),
             device_id_type=MESH_ID,
         )
 
-    def p3(j, half):
-        return pltpu.make_async_remote_copy(
-            src_ref=p1r.at[j % D1, half, rows_at(z * 96 + (1 - other_at[half]) * 48, 48)],
-            dst_ref=p3r.at[j % D3, half],
-            send_sem=p3s_sem.at[j % D3, half],
-            recv_sem=p3r_sem.at[j % D3, half],
-            device_id=other_dev[half],
-            device_id_type=MESH_ID,
-        )
-
-    def add_into(dst, rows, other):
-        dst[rows, :] = (dst[rows, :].astype(F32) + other.astype(F32)).astype(BF16)
+    def total_of(a, b):
+        return (a[...].astype(F32) + b[...].astype(F32)).astype(BF16)
 
     def step0(j):
+        _, pair = job_of(j)
+        for half in range(2):
+            p1s[j % DS, half] = product(half, pair * 2 + half, 1 - first_at[half]).astype(BF16)
+            p1(j, half).start()
+
+    def step1(j):
         e_of, pair = job_of(j)
-        for e in range(2):
-
-            @pl.when(e_of == e)
+
+        @pl.when(e_of == 1)
+        def _():
+            for half in range(2):
+                p1(j, half).wait()
+            for half in range(2):
+                own = product(half, pair * 2 + half, first_at[half])
+                p1r[j % D1, half] = (own + p1r[j % D1, half].astype(F32)).astype(BF16)
+
+        for p in range(6):
+
+            @pl.when(jnp.logical_and(e_of == 0, pair == p))
             def _():
                 for half in range(2):
-                    p1s[j % DS, half] = product(e, half, pair * 2 + half, 1 - first_at[half]).astype(BF16)
-                    p1(j, half).start()
-
-    def step1(j):
-        e_of, pair = job_of(j)
+                    if p in (0, 2):
+                        left_factor(half, p // 2).wait()
+                    elif p == 4:
+                        left_factor(half, 2 + half).wait()
+                    elif p == 5 and half == 0:
+                        left_factor(0, 3).wait()
+                    right_factor(half, p).wait()
+                    p1r[j % D1, half] = pair_product(half, p).astype(BF16)
+
+    def turn(j):
         for half in range(2):
-            p1(j, half).wait()
-        for e in range(2):
-
-            @pl.when(e_of == e)
-            def _():
-                for half in range(2):
-                    own = product(e, half, pair * 2 + half, first_at[half])
-                    p1r[j % D1, half] = (own + p1r[j % D1, half].astype(F32)).astype(BF16)
-
+            other(j, half, False).start()
+
+    def turned(j):
+        for half in range(2):
+            other(j, half, False).wait()
+            mine = p2r.at[j % D2, half]
+            mine[...] = total_of(mine, p1r.at[j % D1, half, :, other_at[half]])
+
+    def ends(j, line_first):
         @pl.when(z == 0)
         def _():
             for half in range(2):
                 for d in (3, 2, 1):
-                    along(j, half, d, True, False).start()
+                    along(j, half, d, True, False, line_first).start()
 
         @pl.when(z == 3)
         def _():
             for half in range(2):
                 for d in (0, 1, 2):
-                    along(j, half, d, False, False).start()
-
-    def relay(j, half, d, right):
-        buf = zr if right else zl
-        along(j, half, d, right, True).wait_recv()
-        add_into(buf.at[j % DZ, half, d], slice(None), p1r[j % D1, half, pl.ds(d * 96, 96), :])
-        along(j, half, d, right, True).start()
-
-    def step2(j):
+                    along(j, half, d, False, False, line_first).start()
+
+    def relay(j, half, d, right, line_first):
+        held = block(zr if right else zl, j, half, d, line_first)
+        along(j, half, d, right, True, line_first).wait_recv()
+        held[...] = total_of(held, own_block(j, half, d, line_first))
+        along(j, half, d, right, True, line_first).start()
+
+    def middle1(j, line_first):
         @pl.when(z == 1)
         def _():
             for half in range(2):
                 for d in (3, 2):
-                    relay(j, half, d, True)
+                    relay(j, half, d, True, line_first)
 
         @pl.when(z == 2)
         def _():
             for half in range(2):
                 for d in (0, 1):
-                    relay(j, half, d, False)
-
-    def step3(j):
+                    relay(j, half, d, False, line_first)
+
+    def middle2(j, line_first):
         @pl.when(z == 2)
         def _():
             for half in range(2):
-                relay(j, half, 3, True)
+                relay(j, half, 3, True, line_first)
 
         @pl.when(z == 1)
         def _():
             for half in range(2):
-                relay(j, half, 0, False)
-
-    def step4(j):
+                relay(j, half, 0, False, line_first)
+
+    def line_end(j, line_first):
         for half in range(2):
-            mine = p1r.at[j % D1, half]
-            rows = rows_at(z * 96, 96)
+            mine = own_block(j, half, z, line_first)
 
             @pl.when(z > 0)
             def _():
-                along(j, half, z, True, True).wait_recv()
-                add_into(mine, rows, zr[j % DZ, half, z])
+                along(j, half, z, True, True, line_first).wait_recv()
+                mine[...] = total_of(mine, block(zr, j, half, z, line_first))
 
             @pl.when(z < 3)
             def _():
-                along(j, half, z, False, True).wait_recv()
-                add_into(mine, rows, zl[j % DZ, half, z])
-
-            p3(j, half).start()
+                along(j, half, z, False, True, line_first).wait_recv()
+                mine[...] = total_of(mine, block(zl, j, half, z, line_first))
+
             for d in range(4):
 
                 @pl.when(d > z)
                 def _():
-                    along(j, half, d, True, True).wait_send()
+                    along(j, half, d, True, True, line_first).wait_send()
 
                 @pl.when(d < z)
                 def _():
-                    along(j, half, d, False, True).wait_send()
+                    along(j, half, d, False, True, line_first).wait_send()
+
+    def pass_on(j):
+        for half in range(2):
+            other(j, half, True).start()
+
+    def passed(j):
+        for half in range(2):
+            other(j, half, True).wait()
 
     def result(slot, half, to):
         return pltpu.make_async_copy(fin.at[slot, half], to, fin_sem.at[slot, half])
 
-    def step5(j):
+    def output(j, line_first):
         e_of, pair = job_of(j)
         for half in range(2):
-            p3(j, half).wait()
-            rows = rows_at(z * 96 + other_at[half] * 48, 48)
-            total = p1r[j % D1, half, rows, :].astype(F32) + p3r[j % D3, half].astype(F32)
 
             @pl.when(j >= 2)
             def _():
                 result(j % 2, half, g_out.at[0]).wait()
 
+            if line_first:
+                total = p1r[j % D1, half, z, other_at[half]].astype(F32) + p2r[j % D2, half, 0].astype(F32)
+            else:
+                total = p2r[j % D2, half, z].astype(F32)
             fin[j % 2, half] = total
             for e in range(2):
                 for p in range(6):
@@ -1047,37 +1178,106 @@
                 low, high = feed_own[at + 1 : at + 2, 0:96], feed_own[at + 2 : at + 3, 0:96]
                 sm_out[at + 2 : at + 3, 0:96] = jnp.where(me < 8, low, high)
 
-    def both(body):
-        body(0, 0)
-        blocks(1, lambda b: body(1, b))
-
-    def all_token_end():
-        both(token_end)
+    def q_second_back():
+        second_back(0, 0)
+        left_factor(0, 0).start()
+        left_factor(1, 0).start()
+
+    def q_feed_back():
+        feed_back(0, 0)
+        for axis in range(2):
+            for pair in (2, 3):
+                right_factor(axis, pair).start()
+
+    def q_first_back():
+        first_back(0, 0)
+        left_factor(0, 2).start()
+
+    def q_attend_back():
+        attend_back(0, 0)
+        right_factor(1, 4).start()
+        right_factor(0, 5).start()
+        right_factor(1, 5).start()
+
+    def q_token_end():
+        token_end(0, 0)
         pltpu.make_async_copy(obq, gq_out, out_sem.at[0]).start()
+
+    def p_token_end():
+        blocks(1, lambda b: token_end(1, b))
         pltpu.make_async_copy(obp, gp_out, out_sem.at[1]).start()
 
-    def wait_out():
-        pltpu.make_async_copy(obq, oq_out, out_sem.at[0]).wait()
-        pltpu.make_async_copy(obp, op_out, out_sem.at[1]).wait()
+    def p_mid(b):
+        first_norm(1, b)
+        feed(1, b)
+
+    def p_second():
+        blocks(1, lambda b: second_norm(1, b))
+        out_p.start()
+
+    def passages(piece):
+        return lambda: blocks(1, lambda b: piece(1, b))
 
     work = {
-        0: [lambda: second_back(0, 0)],
-        1: [lambda: blocks(1, lambda b: second_back(1, b))],
-        2: [lambda: feed_back(0, 0)],
-        3: [lambda: blocks(1, lambda b: feed_back(1, b)), wait_out],
-        4: [lambda: first_back(0, 0)],
-        5: [lambda: blocks(1, lambda b: first_back(1, b))],
-        6: [lambda: attend_back(0, 0)],
-        7: [lambda: blocks(1, lambda b: attend_back(1, b))],
-        8: [lambda: both(token_back)],
-        9: [all_token_end],
+        0: [q_feed_back, lambda: attend(1, 1)],
+        1: [q_first_back, lambda: p_mid(0)],
+        2: [q_attend_back, lambda: p_mid(1)],
+        3: [lambda: token_back(0, 0), p_second, out_q.wait],
+        4: [q_token_end, passages(second_back)],
+        5: [passages(feed_back)],
+        6: [passages(first_back)],
+        7: [passages(attend_back)],
+        8: [passages(token_back)],
+        9: [out_p.wait, p_token_end],
         10: [small_first],
         11: [lambda: small_next(0)],
         12: [lambda: small_next(1)],
         13: [lambda: small_next(2)],
         14: [lambda: small_next(3)],
     }
-    steps = (step1, step2, step3, step4, step5)
+
+    def is_line_first(j):
+        found = j == LINE_FIRST[0]
+        for k in LINE_FIRST[1:]:
+            found = jnp.logical_or(found, j == k)
+        return found
+
+    def steps(late, j):
+        line_first = is_line_first(j)
+        if late == 1:
+            step1(j)
+
+        @pl.when(line_first)
+        def _():
+            if late == 1:
+                ends(j, True)
+            elif late == 2:
+                middle1(j, True)
+            elif late == 3:
+                middle2(j, True)
+            elif late == 4:
+                line_end(j, True)
+                pass_on(j)
+            else:
+                passed(j)
+                output(j, True)
+
+        @pl.when(jnp.logical_not(line_first))
+        def _():
+            if late == 1:
+                turn(j)
+            elif late == 2:
+                turned(j)
+                ends(j, False)
+            elif late == 3:
+                middle1(j, False)
+            elif late == 4:
+                middle2(j, False)
+            else:
+                line_end(j, False)
+                output(j, False)
+
+    q_second_back()
 
     @pl.loop(0, JOBS + 5)
     def _(tick):
@@ -1088,7 +1288,7 @@
                 for thing in things:
                     thing()
 
-        @pl.when(tick < JOBS)
+        @pl.when(jnp.logical_and(tick >= 6, tick < JOBS))
         def _():
             step0(tick)
 
@@ -1096,7 +1296,7 @@
 
             @pl.when(jnp.logical_and(tick >= late, tick < JOBS + late))
             def _():
-                steps[late - 1](tick - late)
+                steps(late, tick - late)
 
     pltpu.make_async_copy(obq, gq_out, out_sem.at[0]).wait()
     pltpu.make_async_copy(obp, gp_out, out_sem.at[1]).wait()
@@ -1183,7 +1383,7 @@
             *both(lambda m: (m, D), BF16),
             *both(lambda m: (m, COLS), BF16),
             *both(lambda m: (m, 12 * COLS), BF16),
-            *both(lambda m: (4 * D, m), BF16),
+            *both(lambda m: (4, ZN, 2, 2, ROWS_OUT, m), BF16),
             *both(lambda m: (m, D), BF16),
             *both(lambda m: (2, m, D), BF16),
             pltpu.VMEM((16, D), F32),
@@ -1198,12 +1398,18 @@
             pltpu.VMEM((2, 8, FF_HERE), F32),
             pltpu.VMEM((4, SMALL, D), F32),
             pltpu.VMEM((4, SMALL, D), F32),
-            pltpu.VMEM((DS, 2, COLS, COLS), BF16),
-            pltpu.VMEM((D1, 2, COLS, COLS), BF16),
-            pltpu.VMEM((DZ, 2, ZN, 96, COLS), BF16),
-            pltpu.VMEM((DZ, 2, ZN, 96, COLS), BF16),
-            pltpu.VMEM((D3, 2, ROWS_OUT, COLS), BF16),
+            pltpu.VMEM((DS, 2, ZN, 2, ROWS_OUT, COLS), BF16),
+            pltpu.VMEM((D1, 2, ZN, 2, ROWS_OUT, COLS), BF16),
+            pltpu.VMEM((D2, 2, ZN, ROWS_OUT, COLS), BF16),
+            pltpu.VMEM((DZ, 2, ZN, 2, ROWS_OUT, COLS), BF16),
+            pltpu.VMEM((DZ, 2, ZN, 2, ROWS_OUT, COLS), BF16),
             pltpu.VMEM((2, 2, ROWS_OUT, COLS), F32),
+            pltpu.VMEM((2, 4, ZN, 2, ROWS_OUT, TOKS[0]), BF16),
+            pltpu.VMEM((2, 6, TOKS[0], COLS), BF16),
+            pltpu.VMEM((2, 16, D), BF16),
+            pltpu.VMEM((2, 16, D), BF16),
+            pltpu.VMEM((16, D), BF16),
+            pltpu.VMEM((16, FF_HERE), BF16),
             dma((2, 2)),
             dma((16,)),
             dma((2,)),
@@ -1215,12 +1421,18 @@
             dma((4,)),
             dma((DS, 2)),
             dma((D1, 2)),
+            dma((D2, 2)),
+            dma((D2, 2)),
             dma((DZ, 2, ZN)),
             dma((DZ, 2, ZN)),
             dma((DZ, 2, ZN)),
             dma((DZ, 2, ZN)),
-            dma((D3, 2)),
-            dma((D3, 2)),
+            dma((2, 4)),
+            dma((2, 4)),
+            dma((2, 6)),
+            dma((2, 6)),
+            dma((2,)),
+            dma((2,)),
         ],
         compiler_params=pltpu.CompilerParams(
             collective_id=0, has_side_effects=True, vmem_limit_bytes=VMEM_BYTES

time: 183 us -> 154 us (0.84)
  Pallas kernels: 182 us -> 153 us
    pallas_call x1, Pallas kernels: 177 us -> 149 us  [fused(): pl.pallas_call(partial(fused_kernel, last=0), name='fused', in_specs=[any...]
where the time goes in v3:
time: 154 us
  Pallas kernels  153 us (99%)
    pallas_call x1, Pallas kernels, fused(): pl.pallas_call(partial(fused_kernel, last=0), name='fused', in_specs=[any...  149 us
    pallas_call x1, Pallas kernels, fused(): pl.pallas_call(finish_kernel, name='finish', in_specs=[any_spec] * 8 + [v...  4.49 us

profile of v3, /device:TPU:0, one launch (start us, length us, event | category | flops | bytes accessed | tf_op | source)
XLA Modules:
  0.0 153.9 jit_solution(11479368121714181560)
XLA Ops:
  0.7 148.6 %fused.1 = (bf16[128,768]{1,0:T(8,128)(2,1)}, bf16[512,768]{1,0:T(8,128)(2,1)}, f32[8,128]{1,0:T(8,128)}, bf16[128,768]{1,0:T(8,128)(2,1)}, bf16[512,768]{1,0:T(...) custom-call(bf16[128,768]{1,0:T(8,128)(2,1)} %bitcast.16, ...), custom_call_target="tpu_custom_call" | custom-call | tf_op jit(solution)/shard_map/fused/pallas_call | solution.py:1349
  149.3 4.5 %finish.1 = (bf16[128,768]{1,0:T(8,128)(2,1)}, bf16[512,768]{1,0:T(8,128)(2,1)}, bf16[128,768]{1,0:T(8,128)(2,1)}, bf16[512,768]{1,0:T(8,128)(2,1)}, f32[2,3,48,...) custom-call(bf16[128,768]{1,0:T(8,128)(2,1)} %get-tuple-element.38.r, ...), custom_call_target="tpu_custom_call" | custom-call | tf_op jit(solution)/shard_map/finish/pallas_call | solution.py:1452

commit v4 on v3

--- a/solution.py
+++ b/solution.py
@@ -368,11 +368,16 @@
 ROWS_OUT = 48
 JOBS = 12
 COLS = 384
-D1, D2, DZ, DS = 8, 6, 5, 2
-LINE_FIRST = (6, 8, 9, 11)
+D1, D2, DZ, DS = 8, 8, 8, 2
+LINE_FIRST = (6, 8, 9)
 TOKS = (128, 512)
 BLK = (128, 256)
 SMALL = 24
+CHUNK = 64
+NORM_UNROLL = (2, 4)
+UP_UNROLL = (6, 6)
+DOWN_UNROLL = (3, 3)
+PAIR_UNROLL = (3, 3)
 
 
 def dot(a, b):
@@ -419,7 +424,7 @@
     win, wo, wf, wd, xq, xp, cq, cp, qkvq, qkvp, prq, prp, hq, hp, n1q, n1p, n2q, n2p,
     i1q, i1p, i2q, i2p, sq, sp, obq, obp, ddq, ddp, dcq, dcp, ballq, ballp, atq, atp,
     exsq, exsp, exrq, exrp, par, pin, pfi, masks, hg, hf, dh, acc_s, acc_b, acc_f, smb, smr,
-    p1s, p1r, p2r, zr, zl, fin, fra, frb, xms, xmr, hm, am,
+    p1s, p1r, p2r, zb, fin, fra, frb, xms, xmr, hm,
     fin_sem, in_sem, out_sem, exs_sem, exr_sem, hgs_sem, hgr_sem, sms_sem, smr_sem,
     p1s_sem, p1r_sem, p2s_sem, p2r_sem, zrs_sem, zrr_sem, zls_sem, zlr_sem,
     fas_sem, far_sem, fbs_sem, fbr_sem, xms_sem, xmr_sem,
@@ -549,7 +554,7 @@
         else:
             seen = col < plen[b]
 
-        @pl.loop(0, 3)
+        @pl.loop(0, 3, unroll=PAIR_UNROLL[e])
         def _(pair):
             q2 = QKV[e][rows, rows_at(pair * 128, 128, 128)]
             k2 = QKV[e][rows, rows_at(COLS + pair * 128, 128, 128)]
@@ -568,12 +573,12 @@
         EXS[e][rows, :] = dot(ctx, wo[e]).astype(BF16)
         exchange(e, b, 0).start()
 
-    CH = 32
+    CH = CHUNK
 
     def first_norm(e, b):
         exchange(e, b, 0).wait()
 
-        @pl.loop(0, BLK[e] // CH)
+        @pl.loop(0, BLK[e] // CH, unroll=NORM_UNROLL[e])
         def _(c):
             rows = rows_at(b * BLK[e] + c * CH, CH, CH)
             v = (
@@ -593,7 +598,7 @@
     def feed(e, b):
         rows = block_rows(e, b)
 
-        @pl.loop(0, 6)
+        @pl.loop(0, 6, unroll=UP_UNROLL[e])
         def _(n):
             cols = rows_at(n * 256, 256, 256)
             u = dot(HID[e][rows, :], wf[e, :, cols]) + pfi[e : e + 1, cols]
@@ -601,7 +606,7 @@
             BALL[e][rows, cols] = a.astype(BF16)
             SLOPE[e][rows, cols] = slope.astype(BF16)
 
-        @pl.loop(0, 3)
+        @pl.loop(0, 3, unroll=DOWN_UNROLL[e])
         def _(n):
             cols = rows_at(n * 256, 256, 256)
             EXS[e][rows, cols] = dot(BALL[e][rows, pl.ds(0, FF_HERE)], wd[e, :, cols]).astype(BF16)
@@ -611,7 +616,7 @@
     def second_norm(e, b):
         exchange(e, b, 1).wait()
 
-        @pl.loop(0, BLK[e] // CH)
+        @pl.loop(0, BLK[e] // CH, unroll=NORM_UNROLL[e])
         def _(c):
             rows = rows_at(b * BLK[e] + c * CH, CH, CH)
             v = (
@@ -672,16 +677,9 @@
     def mini_feed():
         hm[...] = mini_norm(0, first_rows(xp))
 
-        @pl.loop(0, 6)
-        def _(n):
-            cols = rows_at(n * 256, 256, 256)
-            u = dot(hm[...], wf[1, :, cols]) + pfi[1:2, cols]
-            am[:, cols] = gelu_and_slope(u)[0].astype(BF16)
-
-        @pl.loop(0, 3)
-        def _(n):
-            cols = rows_at(n * 256, 256, 256)
-            xms[1, :, cols] = dot(am[...], wd[1, :, cols]).astype(BF16)
+        u = dot(hm[...], wf[1]) + pfi[1:2, :]
+        a = gelu_and_slope(u)[0].astype(BF16)
+        xms[1] = dot(a, wd[1]).astype(BF16)
 
         mini_exchange(1).start()
 
@@ -819,7 +817,7 @@
             group = i if e == 0 else b
             extra = dh[pl.ds(e * 32 + group * 16 + me, 1), :]
 
-            @pl.loop(0, length // CH)
+            @pl.loop(0, length // CH, unroll=NORM_UNROLL[e])
             def _(c):
                 rows = rows_at(group * length + c * CH, CH, CH)
                 add = jnp.where(row0 + c * CH == 0, extra, 0.0)
@@ -838,7 +836,7 @@
     def feed_back(e, b):
         rows = block_rows(e, b)
 
-        @pl.loop(0, 6)
+        @pl.loop(0, 6, unroll=UP_UNROLL[e])
         def _(n):
             cols = rows_at(n * 256, 256, 256)
             d = dot_t(DD[e][rows, :], wd[e, cols, :]) * SLOPE[e][rows, cols].astype(F32)
@@ -846,7 +844,7 @@
             BALL[e][rows, rows_at(4 * COLS + n * 256, 256, 256)] = d
             acc_f[e, :, cols] += fold8(d.astype(F32))
 
-        @pl.loop(0, 3)
+        @pl.loop(0, 3, unroll=DOWN_UNROLL[e])
         def _(n):
             cols = rows_at(n * 256, 256, 256)
             EXS[e][rows, cols] = dot_t(BALL[e][rows, pl.ds(4 * COLS, FF_HERE)], wf[e, cols, :]).astype(BF16)
@@ -858,7 +856,7 @@
     def first_back(e, b):
         exchange(e, b, 0).wait()
 
-        @pl.loop(0, BLK[e] // CH)
+        @pl.loop(0, BLK[e] // CH, unroll=NORM_UNROLL[e])
         def _(c):
             rows = rows_at(b * BLK[e] + c * CH, CH, CH)
             d = N2[e][rows, :] + (EXS[e][rows, :].astype(F32) + EXR[e][0, rows, :].astype(F32))
@@ -878,7 +876,7 @@
         size = BLK[e]
         DC[e][rows, :] = dot_t(DD[e][rows, :], wo[e]).astype(BF16)
 
-        @pl.loop(0, 3)
+        @pl.loop(0, 3, unroll=PAIR_UNROLL[e])
         def _(pair):
             q2 = QKV[e][rows, rows_at(pair * 128, 128, 128)]
             k2 = QKV[e][rows, rows_at(COLS + pair * 128, 128, 128)]
@@ -911,7 +909,7 @@
     def token_back(e, b):
         rows = block_rows(e, b)
 
-        @pl.loop(0, 3)
+        @pl.loop(0, 3, unroll=DOWN_UNROLL[e])
         def _(n):
             cols = rows_at(n * 256, 256, 256)
             EXS[e][rows, cols] = dot_t(BALL[e][rows, pl.ds(9 * COLS, 3 * COLS)], win[e, cols, :]).astype(BF16)
@@ -921,7 +919,7 @@
     def token_end(e, b):
         exchange(e, b, 1).wait()
 
-        @pl.loop(0, BLK[e] // CH)
+        @pl.loop(0, BLK[e] // CH, unroll=NORM_UNROLL[e])
         def _(c):
             rows = rows_at(b * BLK[e] + c * CH, CH, CH)
             OB[e][rows, :] = (
@@ -966,18 +964,19 @@
             device_id_type=MESH_ID,
         )
 
-    def block(ref, j, half, d, line_first):
-        return ref.at[j % DZ, half, d] if line_first else ref.at[j % DZ, half, d, 0]
+    def block(j, half, d, right, line_first, at):
+        slot = d if right else jnp.where(d == at, ZN, d)
+        return zb.at[j % DZ, half, slot] if line_first else zb.at[j % DZ, half, slot, 0]
 
     def own_block(j, half, d, line_first):
         return p1r.at[j % D1, half, d] if line_first else p2r.at[j % D2, half, d]
 
     def along(j, half, d, right, relayed, line_first):
-        buf, send, recv = (zr, zrs_sem, zrr_sem) if right else (zl, zls_sem, zlr_sem)
-        there = block(buf, j, half, d, line_first)
+        send, recv = (zrs_sem, zrr_sem) if right else (zls_sem, zlr_sem)
+        here = block(j, half, d, right, line_first, z)
         return pltpu.make_async_remote_copy(
-            src_ref=there if relayed else own_block(j, half, d, line_first),
-            dst_ref=there,
+            src_ref=here if relayed else own_block(j, half, d, line_first),
+            dst_ref=block(j, half, d, right, line_first, z + 1 if right else z - 1),
             send_sem=send.at[j % DZ, half, d],
             recv_sem=recv.at[j % DZ, half, d],
             device_id=at_dp(me + 4 if right else me - 4),
@@ -1042,7 +1041,7 @@
                     along(j, half, d, False, False, line_first).start()
 
     def relay(j, half, d, right, line_first):
-        held = block(zr if right else zl, j, half, d, line_first)
+        held = block(j, half, d, right, line_first, z)
         along(j, half, d, right, True, line_first).wait_recv()
         held[...] = total_of(held, own_block(j, half, d, line_first))
         along(j, half, d, right, True, line_first).start()
@@ -1078,12 +1077,12 @@
             @pl.when(z > 0)
             def _():
                 along(j, half, z, True, True, line_first).wait_recv()
-                mine[...] = total_of(mine, block(zr, j, half, z, line_first))
+                mine[...] = total_of(mine, block(j, half, z, True, line_first, z))
 
             @pl.when(z < 3)
             def _():
                 along(j, half, z, False, True, line_first).wait_recv()
-                mine[...] = total_of(mine, block(zl, j, half, z, line_first))
+                mine[...] = total_of(mine, block(j, half, z, False, line_first, z))
 
             for d in range(4):
 
@@ -1219,21 +1218,17 @@
         return lambda: blocks(1, lambda b: piece(1, b))
 
     work = {
-        0: [q_feed_back, lambda: attend(1, 1)],
-        1: [q_first_back, lambda: p_mid(0)],
-        2: [q_attend_back, lambda: p_mid(1)],
-        3: [lambda: token_back(0, 0), p_second, out_q.wait],
-        4: [q_token_end, passages(second_back)],
-        5: [passages(feed_back)],
-        6: [passages(first_back)],
-        7: [passages(attend_back)],
-        8: [passages(token_back)],
-        9: [out_p.wait, p_token_end],
-        10: [small_first],
-        11: [lambda: small_next(0)],
-        12: [lambda: small_next(1)],
-        13: [lambda: small_next(2)],
-        14: [lambda: small_next(3)],
+        1: [q_feed_back, lambda: attend(1, 1)],
+        2: [q_first_back, lambda: p_mid(0), q_attend_back, lambda: p_mid(1)],
+        3: [lambda: token_back(0, 0), p_second, out_q.wait, q_token_end, passages(second_back)],
+        4: [passages(feed_back)],
+        7: [passages(first_back), passages(attend_back)],
+        9: [passages(token_back)],
+        11: [small_first],
+        12: [out_p.wait, p_token_end, lambda: small_next(0)],
+        13: [lambda: small_next(1)],
+        14: [lambda: small_next(2)],
+        15: [lambda: small_next(3)],
     }
 
     def is_line_first(j):
@@ -1292,7 +1287,7 @@
         def _():
             step0(tick)
 
-        for late in (5, 4, 3, 2, 1):
+        for late in (1, 2, 3, 4, 5):
 
             @pl.when(jnp.logical_and(tick >= late, tick < JOBS + late))
             def _():
@@ -1401,15 +1396,13 @@
             pltpu.VMEM((DS, 2, ZN, 2, ROWS_OUT, COLS), BF16),
             pltpu.VMEM((D1, 2, ZN, 2, ROWS_OUT, COLS), BF16),
             pltpu.VMEM((D2, 2, ZN, ROWS_OUT, COLS), BF16),
-            pltpu.VMEM((DZ, 2, ZN, 2, ROWS_OUT, COLS), BF16),
-            pltpu.VMEM((DZ, 2, ZN, 2, ROWS_OUT, COLS), BF16),
+            pltpu.VMEM((DZ, 2, ZN + 1, 2, ROWS_OUT, COLS), BF16),
             pltpu.VMEM((2, 2, ROWS_OUT, COLS), F32),
             pltpu.VMEM((2, 4, ZN, 2, ROWS_OUT, TOKS[0]), BF16),
             pltpu.VMEM((2, 6, TOKS[0], COLS), BF16),
             pltpu.VMEM((2, 16, D), BF16),
             pltpu.VMEM((2, 16, D), BF16),
             pltpu.VMEM((16, D), BF16),
-            pltpu.VMEM((16, FF_HERE), BF16),
             dma((2, 2)),
             dma((16,)),
             dma((2,)),

time: 154 us -> 133 us (0.86)
  Pallas kernels: 153 us -> 132 us
    pallas_call x1, Pallas kernels: 149 us -> 127 us  [fused(): pl.pallas_call(partial(fused_kernel, last=0), name='fused', in_specs=[any...]
where the time goes in v4:
time: 133 us
  Pallas kernels  132 us (99%)
    pallas_call x1, Pallas kernels, fused(): pl.pallas_call(partial(fused_kernel, last=0), name='fused', in_specs=[any...  127 us
    pallas_call x1, Pallas kernels, fused(): pl.pallas_call(finish_kernel, name='finish', in_specs=[any_spec] * 8 + [v...  4.49 us

profile of v4, /device:TPU:0, one launch (start us, length us, event | category | flops | bytes accessed | tf_op | source)
XLA Modules:
  0.0 132.7 jit_solution(14539105812336732717)
XLA Ops:
  0.7 127.4 %fused.1 = (bf16[128,768]{1,0:T(8,128)(2,1)}, bf16[512,768]{1,0:T(8,128)(2,1)}, f32[8,128]{1,0:T(8,128)}, bf16[128,768]{1,0:T(8,128)(2,1)}, bf16[512,768]{1,0:T(...) custom-call(bf16[128,768]{1,0:T(8,128)(2,1)} %bitcast.16, ...), custom_call_target="tpu_custom_call" | custom-call | tf_op jit(solution)/shard_map/fused/pallas_call | solution.py:1344
  128.0 4.5 %finish.1 = (bf16[128,768]{1,0:T(8,128)(2,1)}, bf16[512,768]{1,0:T(8,128)(2,1)}, bf16[128,768]{1,0:T(8,128)(2,1)}, bf16[512,768]{1,0:T(8,128)(2,1)}, f32[2,3,48,...) custom-call(bf16[128,768]{1,0:T(8,128)(2,1)} %get-tuple-element.38.r, ...), custom_call_target="tpu_custom_call" | custom-call | tf_op jit(solution)/shard_map/finish/pallas_call | solution.py:1445

commit v5 on v4

--- a/solution.py
+++ b/solution.py
@@ -418,14 +418,15 @@
 
 
 def fused_kernel(
-    xq_in, xp_in, cq_in, cp_in, qlen, plen, dsid, posi,
-    win_in, bin_in, wo_in, wf_in, bfi_in, wd_in, bo_in, gain_in, shift_in,
-    oq_out, op_out, loss_out, gq_out, gp_out, g_in, g_out, g_fi, g_fo, sm_out,
+    xq_in, xp_in, cq_in, cp_in, qlen_in, plen_in, dsid_in, posi_in,
+    win_in, bin_from, wo_in, wf_in, bfi_from, wd_in, bo_from, gain_from, shift_from,
+    oq_out, op_out, gq_out, gp_out, g_in, g_out, g_fi, g_fo, sm_out,
     win, wo, wf, wd, xq, xp, cq, cp, qkvq, qkvp, prq, prp, hq, hp, n1q, n1p, n2q, n2p,
     i1q, i1p, i2q, i2p, sq, sp, obq, obp, ddq, ddp, dcq, dcp, ballq, ballp, atq, atp,
     exsq, exsp, exrq, exrp, par, pin, pfi, masks, hg, hf, dh, acc_s, acc_b, acc_f, smb, smr,
     p1s, p1r, p2r, zb, fin, fra, frb, xms, xmr, hm,
-    fin_sem, in_sem, out_sem, exs_sem, exr_sem, hgs_sem, hgr_sem, sms_sem, smr_sem,
+    qlen, plen, dsid, posi, bin_in, bfi_in, bo_in, gain_in, shift_in, sm,
+    fin_sem, little_sem, in_sem, out_sem, exs_sem, exr_sem, hgs_sem, hgr_sem, sms_sem, smr_sem,
     p1s_sem, p1r_sem, p2s_sem, p2r_sem, zrs_sem, zrr_sem, zls_sem, zlr_sem,
     fas_sem, far_sem, fbs_sem, fbr_sem, xms_sem, xmr_sem,
     *, last,
@@ -445,6 +446,11 @@
     OB, DD, DC, BALL, AT = (obq, obp), (ddq, ddp), (dcq, dcp), (ballq, ballp), (atq, atp)
     EXS, EXR = (exsq, exsp), (exrq, exrp)
 
+    little = [
+        (qlen_in, qlen), (plen_in, plen), (bin_from, bin_in), (bfi_from, bfi_in), (bo_from, bo_in),
+        (gain_from, gain_in), (shift_from, shift_in), (dsid_in, dsid), (posi_in, posi),
+    ]
+    little = [pltpu.make_async_copy(s, d, little_sem.at[i]) for i, (s, d) in enumerate(little)]
     loads = [
         (xq_in, xq),
         *[(win_in.at[0, j], win.at[0, :, pl.ds(j * COLS, COLS)]) for j in range(3)],
@@ -460,7 +466,9 @@
         (cp_in, cp),
     ]
     loads = [pltpu.make_async_copy(s, d, in_sem.at[i]) for i, (s, d) in enumerate(loads)]
-    for copy in loads:
+    for copy in loads[:4]:
+        copy.start()
+    for copy in little:
         copy.start()
     ready = set()
 
@@ -475,6 +483,12 @@
     for k in range(1, 16):
         pl.semaphore_signal(barrier, inc=1, device_id=at_dp(me ^ k), device_id_type=MESH_ID)
 
+    def load(*which):
+        for i in which:
+            loads[i].start()
+
+    for copy in little:
+        copy.wait()
     for e in range(2):
         for i in range(2):
             par[e * 8 + i : e * 8 + i + 1, :] = bo_in[e].astype(F32)[i : i + 1]
@@ -714,17 +728,16 @@
     first_dev, other_dev = (at_x, at_y), (at_y, at_x)
     first_at, other_at = (x, y), (y, x)
 
-    need(0, 1, 2, 3, 8)
+    need(0, 1, 2, 3)
+    load(4, 6, 7, 8, 5, 9, 10, 12, 11, 13, 14, 15)
+    project(0, 0, (0, 1, 2))
+    need(8)
     pl.semaphore_wait(barrier, 16)
-    project(0, 0, (0, 1, 2))
     attend(0, 0)
     right_factor(0, 4).start()
     need(4, 5, 6, 7, 9)
     blocks(1, lambda b: project(1, b, (1, 2)))
     mini_attend()
-    transpose_into(0, 3, xq, 0)
-    left_factor(0, 3).start()
-    left_factor(1, 3).start()
     first_norm(0, 0)
     need(10, 12)
     feed(0, 0)
@@ -733,9 +746,6 @@
             right_factor(axis, pair).start()
     need(11, 13)
     mini_feed()
-    transpose_into(0, 1, hq, 0)
-    left_factor(0, 1).start()
-    left_factor(1, 1).start()
     second_norm(0, 0)
     out_q = pltpu.make_async_copy(obq, oq_out, out_sem.at[0])
     out_p = pltpu.make_async_copy(obp, op_out, out_sem.at[1])
@@ -762,6 +772,12 @@
     for k in range(1, 16):
         heads(k).start()
     need(14, 15)
+    transpose_into(0, 1, hq, 0)
+    for axis in range(2):
+        left_factor(axis, 1).start()
+    transpose_into(0, 3, xq, 0)
+    for axis in range(2):
+        left_factor(axis, 3).start()
     blocks(1, lambda b: project(1, b, (0,)))
     attend(1, 0)
     for k in range(1, 16):
@@ -796,7 +812,7 @@
     log_total = top + jnp.log(jnp.sum(jnp.exp(logits - top), axis=1, keepdims=True))
     target = jnp.sum(chosen * class_scores, axis=1, keepdims=True)
     loss = jnp.sum(log_total - target, axis=0, keepdims=True) * (1.0 / 32)
-    loss_out[...] = jnp.broadcast_to(loss, loss_out.shape)
+    sm[SMALL : SMALL + 8, :] = jnp.broadcast_to(loss, (8, 128))
     d_class = (jnp.exp(logits - log_total) - chosen) * gain
     dh[0:32, :] = lax.dot_general(
         d_class, heads_p, (((1,), (0,)), ((), ())), precision=HIGHEST, preferred_element_type=F32
@@ -1165,17 +1181,18 @@
             small(k + 1).start()
         else:
             total = smb[k] + smr[k]
-            sm_out[...] = jnp.zeros_like(sm_out)
+            sm[0:SMALL, :] = jnp.zeros((SMALL, 128), F32)
             wide = pltpu.roll(total, lax.rem(D - me * ROWS_OUT, D), 1)
-            sm_out[:, 0:ROWS_OUT] = wide[:, 0:ROWS_OUT]
+            sm[0:SMALL, 0:ROWS_OUT] = wide[:, 0:ROWS_OUT]
             heads_own = pltpu.roll(total, lax.rem(D - me * 24, D), 1)
             feed_own = pltpu.roll(total, lax.rem(D - (me % 8) * 96, D), 1)
             for e in range(2):
                 at = e * 9 + 6
                 for i in range(2):
-                    sm_out[at + i : at + i + 1, 0:24] = heads_own[at : at + 1, i * COLS : i * COLS + 24]
+                    sm[at + i : at + i + 1, 0:24] = heads_own[at : at + 1, i * COLS : i * COLS + 24]
                 low, high = feed_own[at + 1 : at + 2, 0:96], feed_own[at + 2 : at + 3, 0:96]
-                sm_out[at + 2 : at + 3, 0:96] = jnp.where(me < 8, low, high)
+                sm[at + 2 : at + 3, 0:96] = jnp.where(me < 8, low, high)
+            pltpu.make_async_copy(sm, sm_out, out_sem.at[2]).start()
 
     def q_second_back():
         second_back(0, 0)
@@ -1295,21 +1312,25 @@
 
     pltpu.make_async_copy(obq, gq_out, out_sem.at[0]).wait()
     pltpu.make_async_copy(obp, gp_out, out_sem.at[1]).wait()
+    pltpu.make_async_copy(sm, sm_out, out_sem.at[2]).wait()
     for slot in range(2):
         for half in range(2):
             result(slot, half, g_out.at[0]).wait()
 
 
 def finish_kernel(*refs):
-    oq, op, gq, gp, g_in, g_out, g_fi, g_fo, loss, sums = refs[:10]
-    large, (loss_to, in_bias, fi_bias, bo, gain, shift) = refs[10:18], refs[18:24]
-    held, in_sems, out_sems = refs[24:32], refs[32], refs[33]
+    oq, op, gq, gp, g_in, g_out, g_fi, g_fo, sums_in = refs[:9]
+    large, (loss_to, in_bias, fi_bias, bo, gain, shift) = refs[9:17], refs[17:23]
+    held, sums, in_sems, out_sems = refs[23:31], refs[31], refs[32], refs[33]
     sources = (oq, op, gq, gp, g_in, g_out, g_fi, g_fo)
     loads = [pltpu.make_async_copy(sources[i], held[i], in_sems.at[i]) for i in range(8)]
     stores = [pltpu.make_async_copy(held[i], large[i], out_sems.at[i]) for i in range(8)]
+    little = pltpu.make_async_copy(sums_in, sums, in_sems.at[8])
+    little.start()
     for load in loads:
         load.start()
-    loss_to[...] = loss[0:1, 0:1]
+    little.wait()
+    loss_to[...] = sums[SMALL : SMALL + 1, 0:1]
     for e in range(2):
         at = e * 9
         gain[e] = sums[at : at + 2, 0:ROWS_OUT]
@@ -1334,7 +1355,6 @@
 ):
     any_spec = pl.BlockSpec(memory_space=pl.ANY)
     vmem = pl.BlockSpec(memory_space=pltpu.VMEM)
-    smem = pl.BlockSpec(memory_space=pltpu.SMEM)
 
     def both(shape, dtype):
         return [pltpu.VMEM(shape(m), dtype) for m in TOKS]
@@ -1344,19 +1364,18 @@
     outs = pl.pallas_call(
         partial(fused_kernel, last=0),
         name="fused",
-        in_specs=[any_spec] * 4 + [smem] * 4 + [any_spec, vmem, any_spec, any_spec, vmem, any_spec] + [vmem] * 3,
-        out_specs=[any_spec, any_spec, vmem] + [any_spec] * 6 + [vmem],
+        in_specs=[any_spec] * 17,
+        out_specs=[any_spec] * 9,
         out_shape=[
             shape((128, D), BF16),
             shape((512, D), BF16),
-            shape((8, 128), F32),
             shape((128, D), BF16),
             shape((512, D), BF16),
             shape((2, 3, ROWS_OUT, COLS), F32),
             shape((2, ROWS_OUT, COLS), F32),
             shape((2, ROWS_OUT, FF_HERE), F32),
             shape((2, ROWS_OUT, FF_HERE), F32),
-            shape((SMALL, 128), F32),
+            shape((SMALL + 8, 128), F32),
         ],
         scratch_shapes=[
             pltpu.VMEM((2, D, 3 * COLS), BF16),
@@ -1403,9 +1422,15 @@
             pltpu.VMEM((2, 16, D), BF16),
             pltpu.VMEM((2, 16, D), BF16),
             pltpu.VMEM((16, D), BF16),
+            *[pltpu.SMEM((n,), jnp.int32) for n in (2, 2, 32, 32)],
+            pltpu.VMEM((2, 2, COLS), BF16),
+            pltpu.VMEM((2, FF_HERE), BF16),
+            *[pltpu.VMEM((2, 2, D), BF16) for _ in range(3)],
+            pltpu.VMEM((SMALL + 8, 128), F32),
             dma((2, 2)),
+            dma((9,)),
             dma((16,)),
-            dma((2,)),
+            dma((3,)),
             dma((3,)),
             dma((2, 3)),
             dma((16,)),
@@ -1439,18 +1464,18 @@
         attn_in.transpose(0, 2, 1, 3), attn_in_bias, attn_out, ffn_in, ffn_in_bias, ffn_out,
         out_biases, norm_gains, norm_shifts,
     )
-    oq, op, loss, gq, gp, g_in, g_out, g_fi, g_fo, sums = outs
+    oq, op, gq, gp, g_in, g_out, g_fi, g_fo, sums = outs
     large = (oq, op, gq, gp, g_in, g_out, g_fi, g_fo)
     small = [(1, 1), (2, 2, 24), (2, 96), (2, 2, ROWS_OUT), (2, 2, ROWS_OUT), (2, 2, ROWS_OUT)]
     oq, op, gq, gp, g_in, g_out, g_fi, g_fo, loss, in_bias, fi_bias, bo, gain, shift = pl.pallas_call(
         finish_kernel,
         name="finish",
-        in_specs=[any_spec] * 8 + [vmem] * 2,
+        in_specs=[any_spec] * 9,
         out_specs=[any_spec] * 8 + [vmem] * 6,
         out_shape=[shape(a.shape, a.dtype) for a in large] + [shape(dims, F32) for dims in small],
-        scratch_shapes=[*[pltpu.VMEM(a.shape, a.dtype) for a in large], dma((8,)), dma((8,))],
+        scratch_shapes=[*[pltpu.VMEM(a.shape, a.dtype) for a in (*large, sums)], dma((9,)), dma((8,))],
         compiler_params=pltpu.CompilerParams(vmem_limit_bytes=VMEM_BYTES),
-    )(*large, loss, sums)
+    )(*large, sums)
     return (
         oq.reshape(2, 64, D),
         op.reshape(2, 256, D),

time: 133 us -> 130 us (0.977)
  Pallas kernels: 132 us -> 129 us
    pallas_call x1, Pallas kernels: 127 us -> 125 us  [fused(): pl.pallas_call(partial(fused_kernel, last=0), name='fused', in_specs=[any...]
where the time goes in v5:
time: 130 us
  Pallas kernels  129 us (99%)
    pallas_call x1, Pallas kernels, fused(): pl.pallas_call(partial(fused_kernel, last=0), name='fused', in_specs=[any...  125 us
    pallas_call x1, Pallas kernels, fused(): pl.pallas_call(finish_kernel, name='finish', in_specs=[any_spec] * 9, out...  3.8 us

profile of v5, /device:TPU:0, one launch (start us, length us, event | category | flops | bytes accessed | tf_op | source)
XLA Modules:
  0.0 129.9 jit_solution(7141714192973535678)
XLA Ops:
  0.7 125.3 %fused.1 = (bf16[128,768]{1,0:T(8,128)(2,1)}, bf16[512,768]{1,0:T(8,128)(2,1)}, bf16[128,768]{1,0:T(8,128)(2,1)}, bf16[512,768]{1,0:T(8,128)(2,1)}, f32[2,3,48,3...) custom-call(bf16[128,768]{1,0:T(8,128)(2,1)} %bitcast.16, ...), custom_call_target="tpu_custom_call" | custom-call | tf_op jit(solution)/shard_map/fused/pallas_call | solution.py:1364
  126.0 3.8 %finish.1 = (bf16[128,768]{1,0:T(8,128)(2,1)}, bf16[512,768]{1,0:T(8,128)(2,1)}, bf16[128,768]{1,0:T(8,128)(2,1)}, bf16[512,768]{1,0:T(8,128)(2,1)}, f32[2,3,48,...) custom-call(bf16[128,768]{1,0:T(8,128)(2,1)} %get-tuple-element.37.r, ...), custom_call_target="tpu_custom_call" | custom-call | tf_op jit(solution)/shard_map/finish/pallas_call | solution.py:1470

commit v6 on v5

--- a/solution.py
+++ b/solution.py
@@ -369,7 +369,7 @@
 JOBS = 12
 COLS = 384
 D1, D2, DZ, DS = 8, 8, 8, 2
-LINE_FIRST = (6, 8, 9)
+LINE_FIRST = (0, 5, 8, 9)
 TOKS = (128, 512)
 BLK = (128, 256)
 SMALL = 24
@@ -1150,7 +1150,7 @@
                             to = g_in.at[e, blk - 9]
                         result(j % 2, half, to).start()
 
-    small_to = (at_x, at_y, at_dp(me ^ 4), at_dp(me ^ 8))
+    small_to = (at_dp(me ^ 8), at_dp(me ^ 4), at_x, at_y)
 
     def small(k):
         return pltpu.make_async_remote_copy(
@@ -1235,17 +1235,19 @@
         return lambda: blocks(1, lambda b: piece(1, b))
 
     work = {
-        1: [q_feed_back, lambda: attend(1, 1)],
-        2: [q_first_back, lambda: p_mid(0), q_attend_back, lambda: p_mid(1)],
-        3: [lambda: token_back(0, 0), p_second, out_q.wait, q_token_end, passages(second_back)],
-        4: [passages(feed_back)],
-        7: [passages(first_back), passages(attend_back)],
-        9: [passages(token_back)],
-        11: [small_first],
-        12: [out_p.wait, p_token_end, lambda: small_next(0)],
-        13: [lambda: small_next(1)],
-        14: [lambda: small_next(2)],
-        15: [lambda: small_next(3)],
+        0: [q_feed_back, lambda: attend(1, 1)],
+        2: [q_first_back, lambda: p_mid(0)],
+        4: [q_attend_back, lambda: p_mid(1)],
+        5: [lambda: token_back(0, 0), p_second, out_q.wait],
+        6: [q_token_end, passages(second_back)],
+        7: [passages(feed_back)],
+        8: [passages(first_back)],
+        9: [passages(attend_back)],
+        10: [passages(token_back), small_first],
+        12: [lambda: small_next(0)],
+        14: [lambda: small_next(1)],
+        15: [out_p.wait, p_token_end, lambda: small_next(2)],
+        16: [lambda: small_next(3)],
     }
 
     def is_line_first(j):

time: 130 us -> 127 us (0.977)
  Pallas kernels: 129 us -> 126 us
    pallas_call x1, Pallas kernels: 125 us -> 122 us  [fused(): pl.pallas_call(partial(fused_kernel, last=0), name='fused', in_specs=[any...]
where the time goes in v6:
time: 127 us
  Pallas kernels  126 us (99%)
    pallas_call x1, Pallas kernels, fused(): pl.pallas_call(partial(fused_kernel, last=0), name='fused', in_specs=[any...  122 us
    pallas_call x1, Pallas kernels, fused(): pl.pallas_call(finish_kernel, name='finish', in_specs=[any_spec] * 9, out...  3.8 us

profile of v6, /device:TPU:0, one launch (start us, length us, event | category | flops | bytes accessed | tf_op | source)
XLA Modules:
  0.0 126.5 jit_solution(3552918148630712088)
XLA Ops:
  0.7 121.9 %fused.1 = (bf16[128,768]{1,0:T(8,128)(2,1)}, bf16[512,768]{1,0:T(8,128)(2,1)}, bf16[128,768]{1,0:T(8,128)(2,1)}, bf16[512,768]{1,0:T(8,128)(2,1)}, f32[2,3,48,3...) custom-call(bf16[128,768]{1,0:T(8,128)(2,1)} %bitcast.16, ...), custom_call_target="tpu_custom_call" | custom-call | tf_op jit(solution)/shard_map/fused/pallas_call | solution.py:1366
  122.6 3.8 %finish.1 = (bf16[128,768]{1,0:T(8,128)(2,1)}, bf16[512,768]{1,0:T(8,128)(2,1)}, bf16[128,768]{1,0:T(8,128)(2,1)}, bf16[512,768]{1,0:T(8,128)(2,1)}, f32[2,3,48,...) custom-call(bf16[128,768]{1,0:T(8,128)(2,1)} %get-tuple-element.37.r, ...), custom_call_target="tpu_custom_call" | custom-call | tf_op jit(solution)/shard_map/finish/pallas_call | solution.py:1472

commit v7 on v6

--- a/solution.py
+++ b/solution.py
@@ -1008,16 +1008,16 @@
             p1s[j % DS, half] = product(half, pair * 2 + half, 1 - first_at[half]).astype(BF16)
             p1(j, half).start()
 
-    def step1(j):
+    def step1(j, send):
         e_of, pair = job_of(j)
 
         @pl.when(e_of == 1)
         def _():
+            own = [product(half, pair * 2 + half, first_at[half]) for half in range(2)]
             for half in range(2):
                 p1(j, half).wait()
-            for half in range(2):
-                own = product(half, pair * 2 + half, first_at[half])
-                p1r[j % D1, half] = (own + p1r[j % D1, half].astype(F32)).astype(BF16)
+                p1r[j % D1, half] = (own[half] + p1r[j % D1, half].astype(F32)).astype(BF16)
+                send(half)
 
         for p in range(6):
 
@@ -1032,29 +1032,23 @@
                         left_factor(0, 3).wait()
                     right_factor(half, p).wait()
                     p1r[j % D1, half] = pair_product(half, p).astype(BF16)
-
-    def turn(j):
-        for half in range(2):
-            other(j, half, False).start()
-
-    def turned(j):
-        for half in range(2):
-            other(j, half, False).wait()
-            mine = p2r.at[j % D2, half]
-            mine[...] = total_of(mine, p1r.at[j % D1, half, :, other_at[half]])
-
-    def ends(j, line_first):
+                    send(half)
+
+    def turned(j, half):
+        other(j, half, False).wait()
+        mine = p2r.at[j % D2, half]
+        mine[...] = total_of(mine, p1r.at[j % D1, half, :, other_at[half]])
+
+    def ends(j, half, line_first):
         @pl.when(z == 0)
         def _():
-            for half in range(2):
-                for d in (3, 2, 1):
-                    along(j, half, d, True, False, line_first).start()
+            for d in (3, 2, 1):
+                along(j, half, d, True, False, line_first).start()
 
         @pl.when(z == 3)
         def _():
-            for half in range(2):
-                for d in (0, 1, 2):
-                    along(j, half, d, False, False, line_first).start()
+            for d in (0, 1, 2):
+                along(j, half, d, False, False, line_first).start()
 
     def relay(j, half, d, right, line_first):
         held = block(j, half, d, right, line_first, z)
@@ -1239,16 +1233,23 @@
         2: [q_first_back, lambda: p_mid(0)],
         4: [q_attend_back, lambda: p_mid(1)],
         5: [lambda: token_back(0, 0), p_second, out_q.wait],
-        6: [q_token_end, passages(second_back)],
-        7: [passages(feed_back)],
-        8: [passages(first_back)],
-        9: [passages(attend_back)],
-        10: [passages(token_back), small_first],
+        6: [q_token_end, lambda: second_back(1, 1)],
+        7: [lambda: feed_back(1, 1)],
+        8: [lambda: first_back(1, 1)],
+        9: [lambda: attend_back(1, 1)],
+        10: [lambda: token_back(1, 1), small_first],
         12: [lambda: small_next(0)],
         14: [lambda: small_next(1)],
         15: [out_p.wait, p_token_end, lambda: small_next(2)],
         16: [lambda: small_next(3)],
     }
+    between = {
+        5: [lambda: second_back(1, 0)],
+        6: [lambda: feed_back(1, 0)],
+        7: [lambda: first_back(1, 0)],
+        8: [lambda: attend_back(1, 0)],
+        9: [lambda: token_back(1, 0)],
+    }
 
     def is_line_first(j):
         found = j == LINE_FIRST[0]
@@ -1259,13 +1260,22 @@
     def steps(late, j):
         line_first = is_line_first(j)
         if late == 1:
-            step1(j)
+
+            def send(half):
+                @pl.when(line_first)
+                def _():
+                    ends(j, half, True)
+
+                @pl.when(jnp.logical_not(line_first))
+                def _():
+                    other(j, half, False).start()
+
+            step1(j, send)
+            return
 
         @pl.when(line_first)
         def _():
-            if late == 1:
-                ends(j, True)
-            elif late == 2:
+            if late == 2:
                 middle1(j, True)
             elif late == 3:
                 middle2(j, True)
@@ -1278,11 +1288,10 @@
 
         @pl.when(jnp.logical_not(line_first))
         def _():
-            if late == 1:
-                turn(j)
-            elif late == 2:
-                turned(j)
-                ends(j, False)
+            if late == 2:
+                for half in range(2):
+                    turned(j, half)
+                    ends(j, half, False)
             elif late == 3:
                 middle1(j, False)
             elif late == 4:
@@ -1311,6 +1320,14 @@
             @pl.when(jnp.logical_and(tick >= late, tick < JOBS + late))
             def _():
                 steps(late, tick - late)
+
+            if late == 2:
+                for at, things in between.items():
+
+                    @pl.when(tick == at)
+                    def _():
+                        for thing in things:
+                            thing()
 
     pltpu.make_async_copy(obq, gq_out, out_sem.at[0]).wait()
     pltpu.make_async_copy(obp, gp_out, out_sem.at[1]).wait()

time: 127 us -> 125 us (0.984)
  Pallas kernels: 126 us -> 124 us
    pallas_call x1, Pallas kernels: 122 us -> 120 us  [fused(): pl.pallas_call(partial(fused_kernel, last=0), name='fused', in_specs=[any...]
where the time goes in v7:
time: 125 us
  Pallas kernels  124 us (99%)
    pallas_call x1, Pallas kernels, fused(): pl.pallas_call(partial(fused_kernel, last=0), name='fused', in_specs=[any...  120 us
    pallas_call x1, Pallas kernels, fused(): pl.pallas_call(finish_kernel, name='finish', in_specs=[any_spec] * 9, out...  3.8 us

profile of v7, /device:TPU:0, one launch (start us, length us, event | category | flops | bytes accessed | tf_op | source)
XLA Modules:
  0.0 124.7 jit_solution(5582667661295367335)
XLA Ops:
  0.7 120.1 %fused.1 = (bf16[128,768]{1,0:T(8,128)(2,1)}, bf16[512,768]{1,0:T(8,128)(2,1)}, bf16[128,768]{1,0:T(8,128)(2,1)}, bf16[512,768]{1,0:T(8,128)(2,1)}, f32[2,3,48,3...) custom-call(bf16[128,768]{1,0:T(8,128)(2,1)} %bitcast.16, ...), custom_call_target="tpu_custom_call" | custom-call | tf_op jit(solution)/shard_map/fused/pallas_call | solution.py:1383
  120.7 3.8 %finish.1 = (bf16[128,768]{1,0:T(8,128)(2,1)}, bf16[512,768]{1,0:T(8,128)(2,1)}, bf16[128,768]{1,0:T(8,128)(2,1)}, bf16[512,768]{1,0:T(8,128)(2,1)}, f32[2,3,48,...) custom-call(bf16[128,768]{1,0:T(8,128)(2,1)} %get-tuple-element.37.r, ...), custom_call_target="tpu_custom_call" | custom-call | tf_op jit(solution)/shard_map/finish/pallas_call | solution.py:1489

commit v8 on v7

--- a/solution.py
+++ b/solution.py
@@ -995,7 +995,7 @@
             dst_ref=block(j, half, d, right, line_first, z + 1 if right else z - 1),
             send_sem=send.at[j % DZ, half, d],
             recv_sem=recv.at[j % DZ, half, d],
-            device_id=at_dp(me + 4 if right else me - 4),
+            device_id=at_dp((me + 4 if right else me + 12) % 16),
             device_id_type=MESH_ID,
         )
 

time: 125 us -> 125 us (level)
  no operation moved by 1% of the time
where the time goes in v8:
time: 125 us; the launch traced here: 124 us
  Pallas kernels  124 us (99%)
    pallas_call x1, Pallas kernels, fused(): pl.pallas_call(partial(fused_kernel, last=0), name='fused', in_specs=[any...  120 us
    pallas_call x1, Pallas kernels, fused(): pl.pallas_call(finish_kernel, name='finish', in_specs=[any_spec] * 9, out...  3.8 us

profile of v8, /device:TPU:0, one launch (start us, length us, event | category | flops | bytes accessed | tf_op | source)
XLA Modules:
  0.0 124.5 jit_solution(4857633812970848513)
XLA Ops:
  0.7 119.8 %fused.1 = (bf16[128,768]{1,0:T(8,128)(2,1)}, bf16[512,768]{1,0:T(8,128)(2,1)}, bf16[128,768]{1,0:T(8,128)(2,1)}, bf16[512,768]{1,0:T(8,128)(2,1)}, f32[2,3,48,3...) custom-call(bf16[128,768]{1,0:T(8,128)(2,1)} %bitcast.16, ...), custom_call_target="tpu_custom_call" | custom-call | tf_op jit(solution)/shard_map/fused/pallas_call | solution.py:1383
  120.5 3.8 %finish.1 = (bf16[128,768]{1,0:T(8,128)(2,1)}, bf16[512,768]{1,0:T(8,128)(2,1)}, bf16[128,768]{1,0:T(8,128)(2,1)}, bf16[512,768]{1,0:T(8,128)(2,1)}, f32[2,3,48,...) custom-call(bf16[128,768]{1,0:T(8,128)(2,1)} %get-tuple-element.37.r, ...), custom_call_target="tpu_custom_call" | custom-call | tf_op jit(solution)/shard_map/finish/pallas_call | solution.py:1489
